TPU v7x, 32 devices: a whole 2x2x4 slice. The times are simulated.
32 devices in a mesh: bucket: 8 (over z, y), mem: 4 (over x, core).
Axes of the slice: x: 2, y: 2, z: 4, core: 2. Of those that a mesh axis runs over, the one named last changes fastest.
Arguments:
- decoder_in: bfloat16 [64, 128, 512], P(('bucket', 'mem')), may hold values from -6 to 6
- memory: bfloat16 [64, 1024, 512], P('bucket', 'mem'), may hold values from -6 to 6
- grad_out: bfloat16 [64, 128, 512], P(('bucket', 'mem')), may hold values from -6 to 6
- decoder_lengths: int32 [64], P(('bucket', 'mem')), may hold values from 1 to 128, as said below
- memory_lengths: int32 [64], P(('bucket', 'mem')), may hold values from 256 to 1024, as said below
- item_route: int32 [64], P(('bucket', 'mem')), may hold values from -1 to 1, as said below
- in_projection: bfloat16 [6, 512, 512], P(None, ('bucket', 'mem')), may hold values from -0.25 to 0.25
- out_projection: bfloat16 [2, 512, 512], P(None, ('bucket', 'mem')), may hold values from -2 to 2
- attention_bias: bfloat16 [6, 512], P(None, ('bucket', 'mem')), may hold values from -3 to 3
- expand_weight: bfloat16 [512, 2048], P(('bucket', 'mem')), may hold values from -0.25 to 0.25
- expand_bias: bfloat16 [2048], P(('bucket', 'mem')), may hold values from -3 to 3
- reduce_weight: bfloat16 [2048, 512], P(None, ('bucket', 'mem')), may hold values from -0.125 to 0.125
- reduce_bias: bfloat16 [512], P(('bucket', 'mem')), may hold values from -3 to 3
- norm_gain: bfloat16 [3, 512], P(None, ('bucket', 'mem')), may hold values from 0.25 to 1.75
- norm_bias: bfloat16 [3, 512], P(None, ('bucket', 'mem')), may hold values from -2 to 2
Outputs:
- decoder_out: bfloat16 [64, 128, 512], P(('bucket', 'mem'))
- grad_decoder: bfloat16 [64, 128, 512], P(('bucket', 'mem'))
- grad_memory: bfloat16 [64, 1024, 512], P('bucket', 'mem')
- grad_in_projection: float32 [6, 512, 512], P(None, ('bucket', 'mem'))
- grad_out_projection: float32 [2, 512, 512], P(None, ('bucket', 'mem'))
- grad_attention_bias: float32 [6, 512], P(None, ('bucket', 'mem'))
- grad_expand_weight: float32 [512, 2048], P(('bucket', 'mem'))
- grad_expand_bias: float32 [2048], P(('bucket', 'mem'))
- grad_reduce_weight: float32 [2048, 512], P(None, ('bucket', 'mem'))
- grad_reduce_bias: float32 [512], P(('bucket', 'mem'))
- grad_norm_gain: float32 [3, 512], P(None, ('bucket', 'mem'))
- grad_norm_bias: float32 [3, 512], P(None, ('bucket', 'mem'))
Inputs may be any that keep to these rules, and one draw needn't show every extreme that they name: `item_route`: -1 marks an empty slot. A value c below 1 means the item is worked on in its own bucket, by the device with the same mem index, in work slot c; a value c of 1 or more means the next bucket (bucket index + 1), same mem index, work slot c - 1. Every work slot of every device receives exactly one item; items of the last bucket stay in it. Some device has no empty slot, and some device receives all its items from the bucket before. `decoder_lengths`: an item's decoder tokens are its first rows; some live item has 128. `memory_lengths`: an item's memory tokens are its first positions; every bucket works on some item with 1024.
All inputs are finite; a program needn't handle non-finite values.
Results may differ from a plain program's by a relative error of at most 0.02.
Values may be sent and summed in bfloat16 or wider, within the bound.
A program may use at most 128 MiB of HBM per device.

v0:
```python
import jax
import jax.numpy as jnp
from jax import lax
from jax.sharding import PartitionSpec as P

HD = 64


EPS = 1e-05
NEG = -1e30


def shifted(value, axis, steps):
    count = lax.axis_size(axis)
    first, last = (max(0, -steps), min(count, count - steps))
    return lax.ppermute(value, axis, [(source, source + steps) for source in range(first, last)])


def layer_norm(value, gain, shift):
    centered = value - jnp.mean(value, axis=-1, keepdims=True)
    spread = jnp.mean(centered * centered, axis=-1, keepdims=True)
    return centered * lax.rsqrt(spread + EPS) * gain + shift


def activate(value):
    return jax.nn.silu(value)


def project(rows_in, weight):
    return jnp.dot(rows_in, weight, preferred_element_type=jnp.float32)


def back_project(grad_rows, weight):
    return jnp.einsum("re,de->rd", grad_rows, weight, preferred_element_type=jnp.float32)


def weight_grad(rows_in, grad_rows):
    return jnp.einsum("rd,re->de", rows_in, grad_rows, preferred_element_type=jnp.float32)


def column_sum(grad_rows):
    return jnp.sum(grad_rows.astype(jnp.float32), axis=0)


def select_items(source, targets, slot_count):
    matches = targets[:, None] == jnp.arange(slot_count, dtype=jnp.int32)[None, :]
    positions = jnp.sum(
        jnp.where(matches, jnp.arange(targets.shape[0], dtype=jnp.int32)[:, None], 0), axis=0
    )
    present = jnp.any(matches, axis=0)
    chosen = jnp.take(source, positions, axis=0)
    shape = (slot_count,) + (1,) * (source.ndim - 1)
    return jnp.where(present.reshape(shape), chosen, jnp.zeros_like(chosen))


def slot_filled(targets, slot_count):
    return jnp.any(targets[:, None] == jnp.arange(slot_count, dtype=jnp.int32)[None, :], axis=0)


def settle(own_part, arrived, filled):
    shape = (filled.shape[0],) + (1,) * (own_part.ndim - 1)
    return jnp.where(filled.reshape(shape), own_part, arrived)


def return_items(results, targets):
    positions = jnp.clip(targets, 0, results.shape[0] - 1)
    chosen = jnp.take(results, positions, axis=0)
    shape = (targets.shape[0],) + (1,) * (results.ndim - 1)
    return jnp.where((targets >= 0).reshape(shape), chosen, jnp.zeros_like(chosen))


def attend_forward(query_rows, key_rows, value_rows, keep_mask, item_count, head_count):
    query_heads = query_rows.reshape(item_count, -1, head_count, HD)
    key_heads = key_rows.reshape(item_count, -1, head_count, HD)
    value_heads = value_rows.reshape(item_count, -1, head_count, HD)
    scores = jnp.einsum(
        "gqhe,gkhe->ghqk", query_heads, key_heads, preferred_element_type=jnp.float32
    ) * HD ** (-0.5)
    scores = jnp.where(keep_mask, scores, NEG)
    row_max = jnp.max(scores, axis=-1, keepdims=True)
    log_total = row_max + jnp.log(jnp.sum(jnp.exp(scores - row_max), axis=-1, keepdims=True))
    weights_low = jnp.exp(scores - log_total).astype(jnp.bfloat16)
    mixed_heads = jnp.einsum(
        "ghqk,gkhe->gqhe", weights_low, value_heads, preferred_element_type=jnp.float32
    )
    return (mixed_heads.reshape(query_rows.shape).astype(jnp.bfloat16), log_total)


def attend_backward(
    query_rows, key_rows, value_rows, keep_mask, log_total, grad_mixed, item_count, head_count
):
    query_heads = query_rows.reshape(item_count, -1, head_count, HD)
    key_heads = key_rows.reshape(item_count, -1, head_count, HD)
    value_heads = value_rows.reshape(item_count, -1, head_count, HD)
    grad_heads = grad_mixed.reshape(item_count, -1, head_count, HD)
    scores = jnp.einsum(
        "gqhe,gkhe->ghqk", query_heads, key_heads, preferred_element_type=jnp.float32
    ) * HD ** (-0.5)
    scores = jnp.where(keep_mask, scores, NEG)
    probabilities = jnp.exp(scores - log_total)
    grad_probs = jnp.einsum(
        "gqhe,gkhe->ghqk", grad_heads, value_heads, preferred_element_type=jnp.float32
    )
    grad_scores = probabilities * (
        grad_probs - jnp.sum(probabilities * grad_probs, axis=-1, keepdims=True)
    )
    scores_low = grad_scores.astype(jnp.bfloat16)
    grad_query = jnp.einsum(
        "ghqk,gkhe->gqhe", scores_low, key_heads, preferred_element_type=jnp.float32
    ) * HD ** (-0.5)
    grad_key = jnp.einsum(
        "ghqk,gqhe->gkhe", scores_low, query_heads, preferred_element_type=jnp.float32
    ) * HD ** (-0.5)
    grad_value = jnp.einsum(
        "ghqk,gqhe->gkhe",
        probabilities.astype(jnp.bfloat16),
        grad_heads,
        preferred_element_type=jnp.float32,
    )
    return (
        grad_query.reshape(query_rows.shape).astype(jnp.bfloat16),
        grad_key.reshape(key_rows.shape).astype(jnp.bfloat16),
        grad_value.reshape(value_rows.shape).astype(jnp.bfloat16),
    )


def shards(
    decoder_in,
    memory,
    grad_out,
    decoder_lengths,
    memory_lengths,
    item_route,
    in_projection,
    out_projection,
    attention_bias,
    expand_weight,
    expand_bias,
    reduce_weight,
    reduce_bias,
    norm_gain,
    norm_bias,
):
    gathered = (
        lax.all_gather(in_projection, ("bucket", "mem"), axis=1, tiled=True),
        lax.all_gather(out_projection, ("bucket", "mem"), axis=1, tiled=True),
        lax.all_gather(attention_bias, ("bucket", "mem"), axis=1, tiled=True),
        lax.all_gather(expand_weight, ("bucket", "mem"), axis=0, tiled=True),
        lax.all_gather(expand_bias, ("bucket", "mem"), axis=0, tiled=True),
        lax.all_gather(reduce_weight, ("bucket", "mem"), axis=1, tiled=True),
        lax.all_gather(reduce_bias, ("bucket", "mem"), axis=0, tiled=True),
        lax.all_gather(norm_gain, ("bucket", "mem"), axis=1, tiled=True),
        lax.all_gather(norm_bias, ("bucket", "mem"), axis=1, tiled=True),
    )
    (
        projections,
        out_weights,
        bias_rows,
        expand_full,
        expand_shift,
        reduce_full,
        reduce_shift,
        gain_rows,
        shift_rows,
    ) = gathered
    bias_rows = bias_rows.astype(jnp.float32)
    expand_shift = expand_shift.astype(jnp.float32)
    reduce_shift = reduce_shift.astype(jnp.float32)
    gain_rows = gain_rows.astype(jnp.float32)
    shift_rows = shift_rows.astype(jnp.float32)
    in_dev = decoder_in.shape[0]
    work_slots = in_dev // 2
    own_target = jnp.where(item_route < work_slots, item_route, -1)
    moved_target = jnp.where(item_route >= work_slots, item_route - work_slots, -1)
    own_filled = slot_filled(own_target, work_slots)
    whole_memory = lax.all_to_all(memory, "mem", split_axis=0, concat_axis=1, tiled=True)
    arrived = shifted(
        (
            select_items(decoder_in, moved_target, work_slots),
            select_items(grad_out, moved_target, work_slots),
            select_items(decoder_lengths, moved_target, work_slots),
            select_items(memory_lengths, moved_target, work_slots),
            select_items(whole_memory, moved_target, work_slots),
        ),
        "bucket",
        1,
    )
    memory_work = settle(select_items(whole_memory, own_target, work_slots), arrived[4], own_filled)
    input_work = settle(select_items(decoder_in, own_target, work_slots), arrived[0], own_filled)
    grad_work = settle(select_items(grad_out, own_target, work_slots), arrived[1], own_filled)
    length_work = settle(
        select_items(decoder_lengths, own_target, work_slots), arrived[2], own_filled
    )
    reach_work = settle(
        select_items(memory_lengths, own_target, work_slots), arrived[3], own_filled
    )
    tokens = lax.psum(jnp.sum(length_work.astype(jnp.float32)), ("bucket", "mem"))
    item_count, dec_span, model_width = input_work.shape
    memory_span = memory_work.shape[1]
    head_count = model_width // HD
    row_count = item_count * dec_span
    input_rows = input_work.reshape(row_count, model_width)
    memory_rows = memory_work.reshape(item_count * memory_span, model_width)
    places = jnp.arange(dec_span)
    keep_self = (places[None, :] <= places[:, None])[None, None] & (
        places[None, None, None, :] < length_work[:, None, None, None]
    )
    keep_cross = jnp.arange(memory_span)[None, None, None, :] < reach_work[:, None, None, None]
    query_rows = (project(input_rows, projections[0]) + bias_rows[0]).astype(jnp.bfloat16)
    key_rows = project(input_rows, projections[1]).astype(jnp.bfloat16)
    value_rows = (project(input_rows, projections[2]) + bias_rows[1]).astype(jnp.bfloat16)
    mixed_rows, total_self = attend_forward(
        query_rows, key_rows, value_rows, keep_self, item_count, head_count
    )
    first_in = input_rows.astype(jnp.float32) + project(mixed_rows, out_weights[0]) + bias_rows[2]
    first_norm, first_pull = jax.vjp(layer_norm, first_in, gain_rows[0], shift_rows[0])
    first_low = first_norm.astype(jnp.bfloat16)
    cross_query = (project(first_low, projections[3]) + bias_rows[3]).astype(jnp.bfloat16)
    cross_keys = project(memory_rows, projections[4]).astype(jnp.bfloat16)
    cross_values = (project(memory_rows, projections[5]) + bias_rows[4]).astype(jnp.bfloat16)
    cross_mixed, total_cross = attend_forward(
        cross_query, cross_keys, cross_values, keep_cross, item_count, head_count
    )
    second_in = first_norm + project(cross_mixed, out_weights[1]) + bias_rows[5]
    second_norm, second_pull = jax.vjp(layer_norm, second_in, gain_rows[1], shift_rows[1])
    second_low = second_norm.astype(jnp.bfloat16)
    hidden_in = project(second_low, expand_full) + expand_shift
    hidden, act_pull = jax.vjp(activate, hidden_in)
    hidden_low = hidden.astype(jnp.bfloat16)
    third_in = second_norm + project(hidden_low, reduce_full) + reduce_shift
    output, third_pull = jax.vjp(layer_norm, third_in, gain_rows[2], shift_rows[2])
    output_work = output.astype(jnp.bfloat16).reshape(item_count, dec_span, model_width)
    live_rows = (places[None, :] < length_work[:, None]).reshape(row_count, 1)
    grad_output = jnp.where(
        live_rows, grad_work.reshape(row_count, model_width).astype(jnp.float32), 0.0
    )
    grad_third, gain_three, shift_three = third_pull(grad_output)
    grad_feed = grad_third.astype(jnp.bfloat16)
    grad_reduce = weight_grad(hidden_low, grad_feed)
    grad_reduce_shift = column_sum(grad_feed)
    grad_hidden = act_pull(back_project(grad_feed, reduce_full))[0].astype(jnp.bfloat16)
    grad_expand = weight_grad(second_low, grad_hidden)
    grad_expand_shift = column_sum(grad_hidden)
    grad_second_out = grad_third + back_project(grad_hidden, expand_full)
    grad_second, gain_two, shift_two = second_pull(grad_second_out)
    grad_cross_out = grad_second.astype(jnp.bfloat16)
    grad_cross_weight = weight_grad(cross_mixed, grad_cross_out)
    grad_cross_shift = column_sum(grad_cross_out)
    grad_cross_mixed = back_project(grad_cross_out, out_weights[1]).astype(jnp.bfloat16)
    grad_cq, grad_ck, grad_cv = attend_backward(
        cross_query,
        cross_keys,
        cross_values,
        keep_cross,
        total_cross,
        grad_cross_mixed,
        item_count,
        head_count,
    )
    memory_grad_rows = back_project(grad_ck, projections[4]) + back_project(grad_cv, projections[5])
    memory_grad_work = memory_grad_rows.astype(jnp.bfloat16).reshape(
        item_count, memory_span, model_width
    )
    grad_first_out = grad_second + back_project(grad_cq, projections[3])
    grad_first, gain_one, shift_one = first_pull(grad_first_out)
    grad_self_out = grad_first.astype(jnp.bfloat16)
    grad_self_weight = weight_grad(mixed_rows, grad_self_out)
    grad_self_shift = column_sum(grad_self_out)
    grad_mixed = back_project(grad_self_out, out_weights[0]).astype(jnp.bfloat16)
    grad_sq, grad_sk, grad_sv = attend_backward(
        query_rows, key_rows, value_rows, keep_self, total_self, grad_mixed, item_count, head_count
    )
    grad_input_rows = (
        grad_first
        + back_project(grad_sq, projections[0])
        + back_project(grad_sk, projections[1])
        + back_project(grad_sv, projections[2])
    )
    input_grad_work = grad_input_rows.astype(jnp.bfloat16).reshape(
        item_count, dec_span, model_width
    )
    grad_projections = jnp.stack(
        [
            weight_grad(input_rows, grad_sq),
            weight_grad(input_rows, grad_sk),
            weight_grad(input_rows, grad_sv),
            weight_grad(first_low, grad_cq),
            weight_grad(memory_rows, grad_ck),
            weight_grad(memory_rows, grad_cv),
        ]
    )
    grad_out_weights = jnp.stack([grad_self_weight, grad_cross_weight])
    grad_biases = jnp.stack(
        [
            column_sum(grad_sq),
            column_sum(grad_sv),
            grad_self_shift,
            column_sum(grad_cq),
            column_sum(grad_cv),
            grad_cross_shift,
        ]
    )
    grad_gains = jnp.stack([gain_one, gain_two, gain_three])
    grad_shifts = jnp.stack([shift_one, shift_two, shift_three])
    summed = (
        lax.psum_scatter(grad_projections, ("bucket", "mem"), scatter_dimension=1, tiled=True),
        lax.psum_scatter(grad_out_weights, ("bucket", "mem"), scatter_dimension=1, tiled=True),
        lax.psum_scatter(grad_biases, ("bucket", "mem"), scatter_dimension=1, tiled=True),
        lax.psum_scatter(grad_expand, ("bucket", "mem"), scatter_dimension=0, tiled=True),
        lax.psum_scatter(grad_expand_shift, ("bucket", "mem"), scatter_dimension=0, tiled=True),
        lax.psum_scatter(grad_reduce, ("bucket", "mem"), scatter_dimension=1, tiled=True),
        lax.psum_scatter(grad_reduce_shift, ("bucket", "mem"), scatter_dimension=0, tiled=True),
        lax.psum_scatter(grad_gains, ("bucket", "mem"), scatter_dimension=1, tiled=True),
        lax.psum_scatter(grad_shifts, ("bucket", "mem"), scatter_dimension=1, tiled=True),
    )
    scaled = tuple((member / tokens for member in summed))
    back = shifted((output_work, input_grad_work, memory_grad_work), "bucket", -1)
    memory_source = return_items(memory_grad_work, own_target) + return_items(back[2], moved_target)
    grad_memory = lax.all_to_all(memory_source, "mem", split_axis=1, concat_axis=0, tiled=True)
    decoder_out = return_items(output_work, own_target) + return_items(back[0], moved_target)
    grad_decoder = return_items(input_grad_work, own_target) + return_items(back[1], moved_target)
    return (
        decoder_out,
        grad_decoder,
        grad_memory,
        scaled[0],
        scaled[1],
        scaled[2],
        scaled[3],
        scaled[4],
        scaled[5],
        scaled[6],
        scaled[7],
        scaled[8],
    )


def solution(mesh):
    in_specs = (
        P(("bucket", "mem"), None, None),
        P("bucket", "mem", None),
        P(("bucket", "mem"), None, None),
        P(("bucket", "mem")),
        P(("bucket", "mem")),
        P(("bucket", "mem")),
        P(None, ("bucket", "mem"), None),
        P(None, ("bucket", "mem"), None),
        P(None, ("bucket", "mem")),
        P(("bucket", "mem"), None),
        P(("bucket", "mem")),
        P(None, ("bucket", "mem")),
        P(("bucket", "mem")),
        P(None, ("bucket", "mem")),
        P(None, ("bucket", "mem")),
    )
    out_specs = (
        P(("bucket", "mem"), None, None),
        P(("bucket", "mem"), None, None),
        P("bucket", "mem", None),
        P(None, ("bucket", "mem"), None),
        P(None, ("bucket", "mem"), None),
        P(None, ("bucket", "mem")),
        P(("bucket", "mem"), None),
        P(("bucket", "mem")),
        P(None, ("bucket", "mem")),
        P(("bucket", "mem")),
        P(None, ("bucket", "mem")),
        P(None, ("bucket", "mem")),
    )
    return jax.shard_map(shards, mesh=mesh, in_specs=in_specs, out_specs=out_specs, check_vma=False)
```

profile of v0, /device:TPU:0, one launch (start us, length us, event | category | flops | bytes accessed | tf_op | source)
XLA Modules:
  0.0 1224.5 jit_solution(11648022122380893058)
XLA Ops:
  9.5 4.2 all-to-all-start
  17.6 1.3 select_select_fusion.8
  18.9 5.0 collective-permute-start
  27.7 4.1 collective-permute-start.1
  33.1 4.7 collective-permute-start.3
  37.8 1.3 select_select_fusion.6
  39.1 4.1 collective-permute-start.5
  43.3 38.6 %all-gather = bf16[32,16,6]{1,2,0:T(8,128)(2,1)S(1)} all-gather(bf16[1,16,6]{1,2,0:T(8,128)(2,1)S(1)} %bitcast.357), channel_id=1, replica_groups=mesh['bucket'=8,'mem'=4] {'bucket','mem'}, dimensions={0}, use_global_device_ids=true | all-gather | bytes 6336 | tf_op jit(solution)/shard_map/all_gather | solution.py:147
  82.2 36.7 %all-gather.1 = bf16[32,16,3]{1,2,0:T(4,128)(2,1)S(1)} all-gather(bf16[1,16,3]{1,2,0:T(4,128)(2,1)S(1)} %bitcast.362), channel_id=1, replica_groups=mesh['bucket'=8,'mem'=4] {'bucket','mem'}, dimensions={0}, use_global_device_ids=true | all-gather | bytes 3168 | tf_op jit(solution)/shard_map/all_gather | solution.py:152
  121.8 38.0 %all-gather.2 = bf16[32,16,3]{1,2,0:T(4,128)(2,1)S(1)} all-gather(bf16[1,16,3]{1,2,0:T(4,128)(2,1)S(1)} %bitcast.363), channel_id=1, replica_groups=mesh['bucket'=8,'mem'=4] {'bucket','mem'}, dimensions={0}, use_global_device_ids=true | all-gather | bytes 3168 | tf_op jit(solution)/shard_map/all_gather | solution.py:153
  160.6 37.2 %all-reduce.5 = (bf16[512]{0:T(512)(128)(2,1)S(1)}, bf16[2048]{0:T(1024)(128)(2,1)S(1)}) all-reduce(bf16[512]{0:T(512)(128)(2,1)S(1)} %dynamic-update-slice.7, bf16[2048]{0:T(1024)(128)(2,1)S(1)} %dynamic-update-slice.6), channel_id=1, replica_groups=mesh['bucket'=8,'mem'=4] {'bucket','mem'}, use_global_device_ids=true, to_apply=%add.1 | all-reduce | flops 2560 | bytes 10240
  200.6 4.4 collective-permute-start.2
  210.3 15.9 %collective-permute-done.2 = bf16[1,1024,512]{2,1,0:T(8,128)(2,1)S(1)} collective-permute-done((bf16[1,1024,512]{2,1,0:T(8,128)(2,1)S(1)}, bf16[1,1024,512]{2,1,0:T(8,128)(2,1)S(1)}, u32[]{:S(2)}, u32[]{:S(2)}) %collective-permute-start.2) | collective-permute-done | bytes 1048608 | tf_op jit(solution)/shard_map/ppermute | solution.py:16
  227.0 1.6 convolution_convert_fusion.6
  228.8 1.3 fusion.13
  230.7 1.3 fusion.12
  232.4 1.4 fusion.74
  234.1 1.3 fusion.14
  235.5 1.8 convolution_convert_fusion.1
  240.3 2.2 add_convert_fusion.1
  244.7 2.1 convolution_add_fusion
  247.0 2.9 fusion.82
  250.1 1.5 fusion.36
  253.1 1.4 convert_reduce_fusion.1
  254.8 1.5 multiply_reduce_fusion.2
  259.0 3.9 multiply_reduce_fusion
  263.0 1.4 multiply_convert_fusion
  264.5 1.6 convert_reduce_fusion.4
  266.1 2.1 multiply_reduce_fusion.3
  272.1 1.5 convert_reduce_fusion.6
  273.7 5.0 convert_reduce_fusion
  283.0 2.2 convolution_bitcast_fusion.1
  288.5 3.1 pad_maximum_fusion
  292.0 1.3 fusion.8
  293.3 1.3 fusion.7
  294.6 2.3 fusion.6
  296.9 2.3 fusion.5
  300.6 1.7 fusion.4
  302.4 1.8 fusion.3
  305.2 2.9 fusion.63
  309.3 2.8 fusion.68
  313.4 1.8 fusion.28
  315.3 1.9 add_convert_fusion
  317.1 1.3 collective-permute-start.7
  318.5 1.3 convolution_add_fusion.3
  319.8 26.6 %collective-permute-done.7 = bf16[1,1024,512]{2,1,0:T(8,128)(2,1)S(1)} collective-permute-done((bf16[1,1024,512]{2,1,0:T(8,128)(2,1)S(1)}, bf16[1,1024,512]{2,1,0:T(8,128)(2,1)S(1)}, u32[]{:S(2)}, u32[]{:S(2)}) %collective-permute-start.7) | collective-permute-done | bytes 1048608 | tf_op jit(solution)/shard_map/ppermute | solution.py:16
  346.5 5.3 fusion.2
  351.8 3.8 all-to-all-start.1
  355.5 1.4 convolution_add_fusion.2
  356.9 1.4 fusion.17
  358.3 1.3 collective-permute-start.6
  359.6 1.3 collective-permute-start.4
  360.9 55.1 %all-reduce.4 = (f32[]{:T(128)}, f32[2048]{0:T(1024)S(1)}, f32[512]{0:T(512)S(1)}) all-reduce(f32[]{:T(128)} %bitcast.114, f32[2048]{0:T(1024)S(1)} %copy-done.73, f32[512]{0:T(512)S(1)} %copy-done.71), channel_id=1, replica_groups=mesh['bucket'=8,'mem'=4] {'bucket','mem'}, use_global_device_ids=true, to_apply=%region_23.28 | all-reduce | flops 2561 | bytes 20488 | tf_op jit(solution)/shard_map/psum | solution.py:197
  420.3 130.8 %reduce-scatter.26.cloned.1.call-done = f32[16,3]{1,0:T(8,128)} async-done(((f32[512,3]{1,0:T(8,128)}), f32[16,3]{1,0:T(8,128)}) %reduce-scatter.26.cloned.1.call-update) | async-done | bytes 208
  554.1 129.1 %reduce-scatter.22.cloned.1.call-done = f32[16,6]{1,0:T(8,128)} async-done(((f32[512,6]{1,0:T(8,128)}), f32[16,6]{1,0:T(8,128)}) %reduce-scatter.22.cloned.1.call-update) | async-done | bytes 400
  686.5 1.5 copy.105
  688.0 130.2 %reduce-scatter.16.cloned.1.call-done = f32[2,16,512]{2,1,0:T(8,128)} async-done(((f32[2,512,512]{2,1,0:T(8,128)}), f32[2,16,512]{2,1,0:T(8,128)}) %reduce-scatter.16.cloned.1.call-update) | async-done | bytes 65552 | tf_op jit(solution)/shard_map/reduce_scatter | solution.py:307
  818.2 2.0 broadcast_divide_fusion.3
  820.2 113.9 %reduce-scatter.14.cloned.1.call-done = f32[6,16,512]{2,1,0:T(8,128)} async-done(((f32[6,512,512]{2,1,0:T(8,128)}), f32[6,16,512]{2,1,0:T(8,128)}) %reduce-scatter.14.cloned.1.call-update) | async-done | bytes 196624 | tf_op jit(solution)/shard_map/reduce_scatter | solution.py:306
  934.1 2.2 broadcast_divide_fusion
  936.3 140.2 %reduce-scatter.18.cloned.1.call-done = f32[16,2048]{1,0:T(8,128)} async-done(((f32[512,2048]{1,0:T(8,128)}), f32[16,2048]{1,0:T(8,128)}) %reduce-scatter.18.cloned.1.call-update) | async-done | bytes 131088 | tf_op jit(solution)/shard_map/reduce_scatter | solution.py:309
  1076.5 2.1 broadcast_divide_fusion.2
  1078.7 137.2 %reduce-scatter.20.cloned.1.call-done = f32[2048,16]{0,1:T(8,128)} async-done(((f32[2048,512]{0,1:T(8,128)}), f32[2048,16]{0,1:T(8,128)}) %reduce-scatter.20.cloned.1.call-update) | async-done | bytes 131088 | tf_op jit(solution)/shard_map/reduce_scatter | solution.py:311
  1215.8 2.1 broadcast_divide_fusion.1
  (333 shorter events, 50.6 us)
Async XLA Ops:
  7.2 6.5 copy-start.99
  7.2 10.4 copy-start.45
  7.2 18.6 %copy-start.92 = (s32[2]{0:T(128)S(1)}, s32[2]{0:T(128)}, u32[]{:S(2)}) copy-start(s32[2]{0:T(128)} %param.27) | copy-start | bytes 28
  7.2 18.6 %copy-start.93 = (s32[2]{0:T(128)S(1)}, s32[2]{0:T(128)}, u32[]{:S(2)}) copy-start(s32[2]{0:T(128)} %param.26) | copy-start | bytes 28
  7.2 30.6 %copy-start.46 = (bf16[2,128,512]{2,1,0:T(8,128)(2,1)S(1)}, bf16[2,128,512]{2,1,0:T(8,128)(2,1)}, u32[]{:S(2)}) copy-start(bf16[2,128,512]{2,1,0:T(8,128)(2,1)} %param.25) | copy-start | bytes 786436
  7.2 36.0 %copy-start.87 = (bf16[6,16]{1,0:T(8,128)(2,1)S(1)}, bf16[6,16]{1,0:T(8,128)(2,1)}, u32[]{:S(2)}) copy-start(bf16[6,16]{1,0:T(8,128)(2,1)} %param.31) | copy-start | bytes 580
  7.2 75.0 %copy-start.95 = (bf16[3,16]{1,0:T(4,128)(2,1)S(1)}, bf16[3,16]{1,0:T(4,128)(2,1)}, u32[]{:S(2)}) copy-start(bf16[3,16]{1,0:T(4,128)(2,1)} %param.36) | copy-start | bytes 292
  7.3 114.5 %copy-start.96 = (bf16[3,16]{1,0:T(4,128)(2,1)S(1)}, bf16[3,16]{1,0:T(4,128)(2,1)}, u32[]{:S(2)}) copy-start(bf16[3,16]{1,0:T(4,128)(2,1)} %param.37) | copy-start | bytes 292
  7.3 152.8 %copy-start.101 = (bf16[16]{0:T(256)(128)(2,1)S(1)}, bf16[16]{0:T(256)(128)(2,1)}, u32[]{:S(2)}) copy-start(bf16[16]{0:T(256)(128)(2,1)} %param.35) | copy-start | bytes 100
  7.3 153.1 %copy-start.102 = (bf16[64]{0:T(256)(128)(2,1)S(1)}, bf16[64]{0:T(256)(128)(2,1)}, u32[]{:S(2)}) copy-start(bf16[64]{0:T(256)(128)(2,1)} %param.33) | copy-start | bytes 388
  7.3 219.7 %all-gather.8.cloned.1.call-start = ((), (), s32[]{:S(2)}) async-start(), calls=%async_computation.9 | async-start | bytes 3244032 | tf_op jit(solution)/shard_map/all_gather | solution.py:145
  8.0 224.3 %all-gather.10.cloned.1.call-start = ((), (), s32[]{:S(2)}) async-start(), calls=%async_computation.10 | async-start | bytes 1081344 | tf_op jit(solution)/shard_map/all_gather | solution.py:146
  8.8 235.9 %all-gather.12.cloned.1.call-start = ((), (), s32[]{:S(2)}) async-start(), calls=%async_computation.11 | async-start | bytes 2162688 | tf_op jit(solution)/shard_map/all_gather | solution.py:148
  9.5 190.1 %all-to-all-start = ((bf16[8,256,512]{2,1,0:T(8,128)(2,1)}), bf16[8,256,512]{2,1,0:T(8,128)(2,1)S(1)}, u32[]{:S(2)}, u32[]{:S(2)}) async-start(bf16[8,256,512]{2,1,0:T(8,128)(2,1)} %param.24), calls=%async_computation | async-start | bytes 4194304 | tf_op jit(solution)/shard_map/all_to_all | solution.py:176
  13.7 233.2 %all-gather.14.cloned.1.call-start = ((), (), s32[]{:S(2)}) async-start(), calls=%async_computation.12 | async-start | bytes 2162688 | tf_op jit(solution)/shard_map/all_gather | solution.py:150
  18.9 190.7 %collective-permute-start = (bf16[1,128,512]{2,1,0:T(8,128)(2,1)}, bf16[1,128,512]{2,1,0:T(8,128)(2,1)}, u32[]{:S(2)}, u32[]{:S(2)}) collective-permute-start(bf16[1,128,512]{2,1,0:T(8,128)(2,1)} %select_select_fusion.8), channel_id=1, source_target_pairs={{0,4},{4,8},{8,12},{12,16},{16,20},{20,24},{24,28},{1,5},{5,9},{9,... | collective-permute-start | bytes 393224 | tf_op jit(solution)/shard_map/ppermute | solution.py:16
  27.7 178.5 %collective-permute-start.1 = (s32[1]{0:T(128)}, s32[1]{0:T(128)}, u32[]{:S(2)}, u32[]{:S(2)}) collective-permute-start(s32[1]{0:T(128)} %select_n.183), channel_id=1, source_target_pairs={{0,4},{4,8},{8,12},{12,16},{16,20},{20,24},{24,28},{1,5},{5,9},{9,... | collective-permute-start | bytes 20 | tf_op jit(solution)/shard_map/ppermute | solution.py:16
  33.1 174.6 %collective-permute-start.3 = (s32[1]{0:T(128)}, s32[1]{0:T(128)}, u32[]{:S(2)}, u32[]{:S(2)}) collective-permute-start(s32[1]{0:T(128)} %select_n.192), channel_id=1, source_target_pairs={{0,4},{4,8},{8,12},{12,16},{16,20},{20,24},{24,28},{1,5},{5,9},{9,... | collective-permute-start | bytes 20 | tf_op jit(solution)/shard_map/ppermute | solution.py:16
  39.1 211.0 %collective-permute-start.5 = (bf16[1,128,512]{2,1,0:T(8,128)(2,1)}, bf16[1,128,512]{2,1,0:T(8,128)(2,1)}, u32[]{:S(2)}, u32[]{:S(2)}) collective-permute-start(bf16[1,128,512]{2,1,0:T(8,128)(2,1)} %select_select_fusion.6), channel_id=1, source_target_pairs={{0,4},{4,8},{8,12},{12,16},{16,20},{20,24},{24,28},{1,5},{5,9},{9,... | collective-permute-start | bytes 393224 | tf_op jit(solution)/shard_map/ppermute | solution.py:16
  43.2 376.3 %reduce-scatter.24.cloned.1.call-start = ((), (), s32[]{:S(2)}) async-start(), calls=%async_computation.18 | async-start | bytes 270336
  200.6 25.5 %collective-permute-start.2 = (bf16[1,1024,512]{2,1,0:T(8,128)(2,1)S(1)}, bf16[1,1024,512]{2,1,0:T(8,128)(2,1)S(1)}, u32[]{:S(2)}, u32[]{:S(2)}) collective-permute-start(bf16[1,1024,512]{2,1,0:T(8,128)(2,1)S(1)} %select_select_fusion), channel_id=1, source_target_pairs={{0,4},{4,8},{8,12},{12,16},{16,20},{20,24},{24,28},{1,5},{5,9},{9,... | collective-permute-start | bytes 3145736 | tf_op jit(solution)/shard_map/ppermute | solution.py:16
  210.2 18.6 %copy-start.91 = (f32[1,512]{1,0:T(1,128)S(1)}, f32[1,512]{1,0:T(1,128)}, u32[]{:S(2)}) copy-start(f32[1,512]{1,0:T(1,128)} %get-tuple-element.122) | copy-start | bytes 6148
  210.2 20.4 %copy-start.90 = (f32[1,512]{1,0:T(1,128)S(1)}, f32[1,512]{1,0:T(1,128)}, u32[]{:S(2)}) copy-start(f32[1,512]{1,0:T(1,128)} %get-tuple-element.123) | copy-start | bytes 6148
  226.9 13.3 %copy-start.32 = (bf16[1,1024,512]{2,1,0:T(8,128)(2,1)}, bf16[1,1024,512]{2,1,0:T(8,128)(2,1)S(1)}, u32[]{:S(2)}) copy-start(bf16[1,1024,512]{2,1,0:T(8,128)(2,1)S(1)} %fusion.26) | copy-start | bytes 3145732
  226.9 5.4 copy-start.69
  228.6 5.4 copy-start.48
  232.1 6.2 copy-start.57
  232.3 6.9 copy-start.26
  233.8 9.9 copy-start.60
  234.0 9.7 copy-start.65
  244.5 10.1 copy-start.63
  244.7 9.9 copy-start.75
  246.9 6.3 copy-start.7
  247.0 6.2 copy-start.100
  254.5 8.4 copy-start.11
  264.5 6.0 copy-start.31
  272.1 6.5 copy-start.38
  272.1 6.5 copy-start.41
  273.7 6.4 copy-start.22
  273.7 6.7 copy-start.67
  273.7 6.7 copy-start.70
  273.7 6.7 copy-start.74
  278.6 7.4 copy-start.59
  280.3 11.6 copy-start.15
  281.3 269.8 %reduce-scatter.26.cloned.1.call-start = ((), (), s32[]{:S(2)}) async-start(), calls=%async_computation.19 | async-start | bytes 270336
  282.9 400.3 %reduce-scatter.22.cloned.1.call-start = ((), (), s32[]{:S(2)}) async-start(), calls=%async_computation.17 | async-start | bytes 270336
  288.5 529.7 %reduce-scatter.16.cloned.1.call-start = ((), (), s32[]{:S(2)}) async-start(), calls=%async_computation.14 | async-start | bytes 2162688 | tf_op jit(solution)/shard_map/reduce_scatter | solution.py:307
  291.6 7.6 copy-start.14
  291.6 642.5 %reduce-scatter.14.cloned.1.call-start = ((), (), s32[]{:S(2)}) async-start(), calls=%async_computation.13 | async-start | bytes 6488064 | tf_op jit(solution)/shard_map/reduce_scatter | solution.py:306
  292.0 7.7 copy-start.17
  294.6 6.1 copy-start.33
  304.2 772.3 %reduce-scatter.18.cloned.1.call-start = ((), (), s32[]{:S(2)}) async-start(), calls=%async_computation.15 | async-start | bytes 4325376 | tf_op jit(solution)/shard_map/reduce_scatter | solution.py:309
  308.1 907.7 %reduce-scatter.20.cloned.1.call-start = ((), (), s32[]{:S(2)}) async-start(), calls=%async_computation.16 | async-start | bytes 4325376 | tf_op jit(solution)/shard_map/reduce_scatter | solution.py:311
  315.2 31.2 %copy-start.79 = (pred[2]{0:T(512)(128)(4,1)S(1)}, pred[2]{0:T(512)(128)(4,1)}, u32[]{:S(2)}) copy-start(pred[2]{0:T(512)(128)(4,1)} %get-tuple-element.136) | copy-start | bytes 10
  315.2 31.2 %copy-start.80 = (pred[2]{0:T(512)(128)(4,1)S(1)}, pred[2]{0:T(512)(128)(4,1)}, u32[]{:S(2)}) copy-start(pred[2]{0:T(512)(128)(4,1)} %get-tuple-element.137) | copy-start | bytes 10
  315.2 31.2 %copy-start.81 = (pred[2]{0:T(512)(128)(4,1)S(1)}, pred[2]{0:T(512)(128)(4,1)}, u32[]{:S(2)}) copy-start(pred[2]{0:T(512)(128)(4,1)} %get-tuple-element.138) | copy-start | bytes 10
  315.2 31.2 %copy-start.82 = (pred[2]{0:T(512)(128)(4,1)S(1)}, pred[2]{0:T(512)(128)(4,1)}, u32[]{:S(2)}) copy-start(pred[2]{0:T(512)(128)(4,1)} %get-tuple-element.139) | copy-start | bytes 10
  317.1 29.3 %collective-permute-start.7 = (bf16[1,1024,512]{2,1,0:T(8,128)(2,1)S(1)}, bf16[1,1024,512]{2,1,0:T(8,128)(2,1)S(1)}, u32[]{:S(2)}, u32[]{:S(2)}) collective-permute-start(bf16[1,1024,512]{2,1,0:T(8,128)(2,1)S(1)} %bitcast.284), channel_id=1, source_target_pairs={{4,0},{8,4},{12,8},{16,12},{20,16},{24,20},{28,24},{5,1},{9,5},{13... | collective-permute-start | bytes 3145736 | tf_op jit(solution)/shard_map/ppermute | solution.py:16
  351.8 7.8 copy-start.42
  351.8 9.1 copy-start.71
  351.8 9.1 copy-start.73
  351.8 334.4 %all-to-all-start.1 = ((bf16[2,1024,512]{2,0,1:T(2,128)(2,1)}), bf16[2,1024,512]{2,0,1:T(2,128)(2,1)S(1)}, u32[]{:S(2)}, u32[]{:S(2)}) async-start(bf16[2,1024,512]{2,0,1:T(2,128)(2,1)} %fusion.2), calls=%async_computation.1 | async-start | bytes 4194304 | tf_op jit(solution)/shard_map/all_to_all | solution.py:319
  358.3 326.9 %collective-permute-start.6 = (bf16[1,128,512]{2,1,0:T(8,128)(2,1)S(1)}, bf16[1,128,512]{2,1,0:T(8,128)(2,1)S(1)}, u32[]{:S(2)}, u32[]{:S(2)}) collective-permute-start(bf16[1,128,512]{2,1,0:T(8,128)(2,1)S(1)} %bitcast.319), channel_id=1, source_target_pairs={{4,0},{8,4},{12,8},{16,12},{20,16},{24,20},{28,24},{5,1},{9,5},{13... | collective-permute-start | bytes 393224 | tf_op jit(solution)/shard_map/ppermute | solution.py:16
  359.6 325.6 %collective-permute-start.4 = (bf16[1,128,512]{2,1,0:T(8,128)(2,1)S(1)}, bf16[1,128,512]{2,1,0:T(8,128)(2,1)S(1)}, u32[]{:S(2)}, u32[]{:S(2)}) collective-permute-start(bf16[1,128,512]{2,1,0:T(8,128)(2,1)S(1)} %bitcast.318), channel_id=1, source_target_pairs={{4,0},{8,4},{12,8},{16,12},{20,16},{24,20},{28,24},{5,1},{9,5},{13... | collective-permute-start | bytes 393224 | tf_op jit(solution)/shard_map/ppermute | solution.py:16
  (60 other events, 153.9 us)
Sparse Core Ops, SparseCore 0:
  11.0 62.7 all-gather.7
  76.8 52.3 all-gather.9
  132.0 55.3 all-gather.11
  190.1 56.1 all-gather.13
  281.4 138.0 reduce-scatter.23
  421.7 129.3 reduce-scatter.25
  553.9 129.3 reduce-scatter.21
  685.6 132.5 reduce-scatter.15
  823.8 110.2 reduce-scatter.13
  936.3 140.1 reduce-scatter.17
  1078.9 136.8 reduce-scatter.19
where the time goes:
time: 1230 us; the launch traced here: 1220 us
  waiting for transfers between devices  827 us (67%)
  blocking collectives  206 us (17%)
  matrix products  66.2 us (5%)
  other arithmetic  41.5 us (3%)
  starting transfers between devices  34.5 us (3%)
  between operations  27.2 us (2%)
  local copies, waits for them, and re-layouts  22.1 us (2%)
    unnamed x14, waiting for transfers between devices  263 us
    reduce_scatter x1, waiting for transfers between devices, shards(): lax.psum_scatter(grad_expand, ('bucket', 'mem'), scatter_dimension=0, til...  140 us
    reduce_scatter x1, waiting for transfers between devices, shards(): lax.psum_scatter(grad_reduce, ('bucket', 'mem'), scatter_dimension=1, til...  137 us
    reduce_scatter x1, waiting for transfers between devices, shards(): lax.psum_scatter(grad_out_weights, ('bucket', 'mem'), scatter_dimension=1...  130 us
    reduce_scatter x1, waiting for transfers between devices, shards(): lax.psum_scatter(grad_projections, ('bucket', 'mem'), scatter_dimension=1...  114 us
    psum x1, blocking collectives, shards(): lax.psum(jnp.sum(length_work.astype(jnp.float32)), ('bucket', 'mem'))  55.1 us
    ppermute x8, waiting for transfers between devices, shifted(): lax.ppermute(value, axis, [(source, source + steps) for source in range(f...  42.5 us
    all_gather x1, blocking collectives, shards(): lax.all_gather(attention_bias, ('bucket', 'mem'), axis=1, tiled=True)  38.6 us
  transfers between devices with their start and end apart: 21, of which 9 were waited for; matrix products, arithmetic and copies ran while one was open for 7% of the time, Pallas kernels for 0%

commit v1 on v0

v1 whole, which is shorter than its diff:
```python
import functools

import jax
import jax.numpy as jnp
from jax import lax
from jax.experimental import pallas as pl
from jax.experimental.pallas import tpu as pltpu
from jax.sharding import PartitionSpec as P

HD = 64
EPS = 1e-05
NEG = -1e30
F32 = jnp.float32
BF16 = jnp.bfloat16
MESH = pl.DeviceIdType.MESH
LANES = 128
ROWS = 16

SQ, SK, SV, SO, CK, CV, CQ, CO, EXPAND, REDUCE = 0, 1, 2, 3, 4, 5, 6, 7, 8, 12
BLOCKS = 16
GATHER_CHUNKS = tuple((low, low + 2, "zxyc") for low in range(0, BLOCKS, 2))
SCATTER_CHUNKS = tuple((low, low + 2, "cyxz") for low in range(BLOCKS - 2, -1, -2))
AXES = "zyxc"


def mm(left, right):
    return lax.dot_general(left, right, (((1,), (0,)), ((), ())), preferred_element_type=F32)


def mm_nt(left, right):
    return lax.dot_general(left, right, (((1,), (1,)), ((), ())), preferred_element_type=F32)


def mm_tn(left, right):
    return lax.dot_general(left, right, (((0,), (0,)), ((), ())), preferred_element_type=F32)


class Links:
    def __init__(self, send_sems, recv_sems):
        self.send_sems, self.recv_sems, self.used, self.sent = send_sems, recv_sems, 0, []

    def pair(self):
        self.used += 1
        return self.send_sems.at[self.used - 1], self.recv_sems.at[self.used - 1]

    def copy(self, source, target, landing, device):
        send, recv = self.pair()
        out = pltpu.make_async_remote_copy(
            src_ref=source, dst_ref=target, send_sem=send, recv_sem=recv,
            device_id=device, device_id_type=MESH,
        )
        out.start()
        self.sent.append(out)
        return pltpu.make_async_remote_copy(
            src_ref=source, dst_ref=landing, send_sem=send, recv_sem=recv,
            device_id=device, device_id_type=MESH,
        )

    def finish(self):
        for out in self.sent:
            out.wait_send()


class Place:
    def __init__(self, sizes):
        self.sizes = sizes
        bucket, mem = lax.axis_index("bucket"), lax.axis_index("mem")
        self.bucket, self.mem = bucket, mem
        self.at = {
            "z": bucket // sizes["y"], "y": bucket % sizes["y"],
            "x": mem // sizes["c"], "c": mem % sizes["c"],
        }

    def shifted(self, axis, step):
        size = self.sizes[axis]
        return lax.rem(self.at[axis] + (step % size), size)

    def device(self, axis, step):
        at = dict(self.at)
        at[axis] = self.shifted(axis, step)
        return (at["z"] * self.sizes["y"] + at["y"], at["x"] * self.sizes["c"] + at["c"])


def block_view(ref, lead, index):
    return ref.at[tuple(lead) + tuple(index[axis] for axis in AXES)]


class Gather:
    def __init__(self, links, place, grid, order, parts):
        self.links, self.place, self.parts = links, place, parts
        self.order = [axis for axis in order if grid[axis] > 1]
        self.grid, self.waits, self.done = grid, [], 0

    def step(self):
        for wait in self.waits:
            wait.wait_recv()
        self.waits = []
        if self.done < len(self.order):
            axis = self.order[self.done]
            known = self.order[: self.done]
            for hop in range(1, self.grid[axis]):
                mine, theirs = {}, {}
                for other in AXES:
                    if other in known:
                        mine[other] = theirs[other] = slice(None)
                    else:
                        at = self.place.at[other] if self.grid[other] > 1 else 0
                        mine[other] = theirs[other] = at
                theirs[axis] = self.place.shifted(axis, -hop)
                for ref, lead in self.parts:
                    self.waits.append(
                        self.links.copy(
                            block_view(ref, lead, mine), block_view(ref, lead, mine),
                            block_view(ref, lead, theirs), self.place.device(axis, hop),
                        )
                    )
        self.done += 1


class Scatter:
    def __init__(self, links, place, grid, order, parts, landings, emit):
        self.links, self.place, self.parts, self.landings = links, place, parts, landings
        self.order = [axis for axis in order if grid[axis] > 1]
        self.grid, self.waits, self.done, self.emit = grid, [], 0, emit

    def index(self, known):
        return {
            axis: (self.place.at[axis] if self.grid[axis] > 1 else 0) if axis in known or self.grid[axis] == 1
            else slice(None)
            for axis in AXES
        }

    def step(self):
        for wait in self.waits:
            wait.wait_recv()
        self.waits = []
        if self.done > 0:
            axis = self.order[self.done - 1]
            last = self.done == len(self.order)
            index = self.index(self.order[: self.done])
            for number, (ref, lead) in enumerate(self.parts):
                where = tuple(lead) + tuple(index[name] for name in AXES)
                total = ref[where].astype(F32)
                for hop in range(1, self.grid[axis]):
                    total += self.landings[number][self.done - 1][hop - 1].astype(F32)
                if last:
                    self.emit[number](total)
                else:
                    ref[where] = total.astype(ref.dtype)
        if self.done < len(self.order):
            axis = self.order[self.done]
            known = self.order[: self.done]
            for hop in range(1, self.grid[axis]):
                theirs = self.index(known)
                theirs[axis] = self.place.shifted(axis, hop)
                for number, (ref, lead) in enumerate(self.parts):
                    landing = self.landings[number][self.done].at[hop - 1]
                    self.waits.append(
                        self.links.copy(
                            block_view(ref, lead, theirs), landing, landing, self.place.device(axis, hop)
                        )
                    )
        self.done += 1


def landing_shapes(grid, order, lead_shape, tail_shape):
    shapes, left = [], {axis: grid[axis] for axis in AXES}
    for axis in order:
        if grid[axis] == 1:
            continue
        left[axis] = 1
        kept = tuple(left[name] for name in AXES if left[name] > 1)
        shapes.append(pltpu.VMEM((grid[axis] - 1,) + lead_shape + kept + tail_shape, BF16))
    return shapes


def layer_kernel(
    sizes, grid,
    lengths_ref, reaches_ref, routes_ref, x_ref, dy_ref, pack_ref, small_ref, memory_ref,
    out_ref, dx_ref, gw_ref, gs_ref, gmem_ref,
    scratch,
):
    s = scratch
    place = Place(sizes)
    links = Links(s["send"], s["recv"])
    slots, span, width = x_ref.shape
    rows = slots * span
    members, chunk = s["mem"].shape[1], s["mem"].shape[2]
    reach_span = members * chunk
    heads = width // HD
    pairs = heads // 2
    ff_blocks = (BLOCKS - EXPAND) // 2

    barrier = pltpu.get_barrier_semaphore()
    peers = []
    for axis in "zy":
        peers += [place.device(axis, hop) for hop in range(1, sizes[axis])]
    others = [lax.rem(place.mem + hop, members) for hop in range(1, members)]
    peers += [(place.bucket, other) for other in others]
    for peer in peers:
        pl.semaphore_signal(barrier, inc=1, device_id=peer, device_id_type=MESH)

    def here(ref, lead=()):
        return block_view(ref, lead, {a: place.at[a] if grid[a] > 1 else 0 for a in AXES})

    own = [
        pltpu.make_async_copy(pack_ref, here(s["w"], (slice(None),)), s["local"].at[0]),
        pltpu.make_async_copy(small_ref, here(s["small"]), s["local"].at[1]),
    ]
    own_memory = pltpu.make_async_copy(
        memory_ref.at[pl.ds(place.mem * slots, slots)], s["mem"].at[:, place.mem], s["local"].at[2]
    )
    for copy in own:
        copy.start()
    own_memory.start()
    for copy in own:
        copy.wait()
    pl.semaphore_wait(barrier, len(peers))

    gathers = []
    for number, (low, high, order) in enumerate(GATHER_CHUNKS):
        parts = [(s["w"], (slice(low, high),))]
        if number == 0:
            parts.append((s["small"], ()))
        gathers.append(Gather(links, place, grid, order, parts))
    memory_waits = []

    def send_memory():
        for hop, other in zip(range(1, members), others):
            sender = lax.rem(place.mem + members - hop, members)
            memory_waits.append(
                links.copy(
                    memory_ref.at[pl.ds(other * slots, slots)], s["mem"].at[:, place.mem],
                    s["mem"].at[:, sender], (place.bucket, other),
                )
            )

    def weight(number):
        return s["w"][number].reshape(width, width)

    def put_grad(number, value):
        ref = s["gw"]
        ref[number] = value.astype(BF16).reshape(ref.shape[1:])

    lane = lax.broadcasted_iota(jnp.int32, (1, LANES), 1)
    even = jnp.where(lane < HD, 1.0, 0.0)
    odd = 1.0 - even
    scale = HD ** (-0.5)

    def stack(value, factor=1.0):
        return jnp.concatenate([value * (even * factor).astype(BF16), value * (odd * factor).astype(BF16)], axis=0)

    def unstack(value, factor=1.0):
        return value[:span] * (even * factor) + value[span:] * (odd * factor)

    def normed(value):
        centered = value - jnp.mean(value, axis=-1, keepdims=True)
        rstd = lax.rsqrt(jnp.mean(centered * centered, axis=-1, keepdims=True) + EPS)
        return centered * rstd, rstd

    def norm_back(grad, unit, rstd, number):
        s["rows_grad"][6 + number : 7 + number, :] = jnp.sum(grad * unit, axis=0, keepdims=True)
        s["rows_grad"][9 + number : 10 + number, :] = jnp.sum(grad, axis=0, keepdims=True)
        scaled = grad * s["rows"][6 + number : 7 + number, :]
        return (
            scaled - jnp.mean(scaled, axis=-1, keepdims=True)
            - unit * jnp.mean(scaled * unit, axis=-1, keepdims=True)
        ) * rstd

    def column_sum(value):
        return jnp.sum(value.astype(F32), axis=0, keepdims=True)

    def bias(number):
        return s["rows"][number : number + 1, :]

    def unpack_small():
        places = width // ROWS
        every = s["small"][...].reshape(places, ROWS, LANES).astype(F32)
        group = LANES // ROWS
        columns = [jnp.sum(every[g * group : (g + 1) * group], axis=0) for g in range(places // group)]
        s["rows"][...] = jnp.concatenate(columns, axis=1)
        share = LANES // (width * ff_blocks // places)
        pieces = [
            jnp.sum(every[g * share : (g + 1) * share, 13], axis=0, keepdims=True) for g in range(places // share)
        ]
        s["ebias"][...] = jnp.concatenate(pieces, axis=1)
        tokens = jnp.sum(jnp.sum(every[:, 14], axis=0, keepdims=True), axis=1, keepdims=True)
        s["tokens"][...] = jnp.broadcast_to(tokens, s["tokens"].shape)

    def self_project():
        x = x_ref[...].reshape(rows, width)
        s["q"][...] = (mm(x, weight(SQ)) + bias(0)).astype(BF16)
        s["k"][...] = mm(x, weight(SK)).astype(BF16)
        s["v"][...] = (mm(x, weight(SV)) + bias(1)).astype(BF16)

    def softmax(scores):
        top = jnp.max(scores, axis=-1, keepdims=True)
        weights = jnp.exp(scores - top)
        return (weights * (1.0 / jnp.sum(weights, axis=-1, keepdims=True))).astype(BF16)

    def self_attend():
        row = lax.broadcasted_iota(jnp.int32, (2 * span, span), 0) % span
        col = lax.broadcasted_iota(jnp.int32, (2 * span, span), 1)
        for slot in range(slots):
            keep = (col <= row) & (col < lengths_ref[slot])
            at = slice(slot * span, (slot + 1) * span)
            for pair in range(pairs):
                lanes = slice(pair * LANES, (pair + 1) * LANES)
                scores = mm_nt(stack(s["q"][at, lanes], scale), s["k"][at, lanes])
                low = softmax(jnp.where(keep, scores, NEG))
                s["ps"][slot, pair] = low
                s["a"][at, lanes] = unstack(mm(low, s["v"][at, lanes])).astype(BF16)

    def self_close():
        x = x_ref[...].reshape(rows, width).astype(F32)
        unit, rstd = normed(x + mm(s["a"][...], weight(SO)) + bias(2))
        s["n1"][...], s["d1"][...] = unit, rstd
        h1 = unit * bias(6) + bias(9)
        s["h1"][...] = h1
        s["h1b"][...] = h1.astype(BF16)

    def cross_query():
        s["q2"][...] = (mm(s["h1b"][...], weight(CQ)) + bias(3)).astype(BF16)

    def cross_memory(slot):
        for which, number in (("k2", CK), ("v2", CV)):
            def body(part, carry, which=which, number=number):
                value = mm(s["mem"][slot, part], weight(number))
                if which == "v2":
                    value = value + bias(4)
                s[which][slot, part] = value.astype(BF16)
                return carry
            lax.fori_loop(0, members, body, 0)

    def keys(name, slot, lanes):
        return s[name][slot, :, :, lanes].reshape(reach_span, LANES)

    def cross_attend(slot):
        col = lax.broadcasted_iota(jnp.int32, (1, reach_span), 1)
        keep = col < reaches_ref[slot]
        at = slice(slot * span, (slot + 1) * span)

        def body(pair, carry):
            lanes = pl.ds(pl.multiple_of(pair * LANES, LANES), LANES)
            scores = mm_nt(stack(s["q2"][at, lanes], scale), keys("k2", slot, lanes))
            low = softmax(jnp.where(keep, scores, NEG))
            s["pc"][slot, pair] = low
            s["a2"][at, lanes] = unstack(mm(low, keys("v2", slot, lanes))).astype(BF16)
            return carry
        lax.fori_loop(0, pairs, body, 0)

    def cross_close():
        unit, rstd = normed(s["h1"][...] + mm(s["a2"][...], weight(CO)) + bias(5))
        s["n2"][...], s["d2"][...] = unit, rstd
        h2 = unit * bias(7) + bias(10)
        s["h2b"][...] = h2.astype(BF16)
        s["r3"][...] = h2 + bias(12)

    def ff_up(block):
        lanes = slice(block * width, (block + 1) * width)
        u = mm(s["h2b"][...], weight(EXPAND + block)) + s["ebias"][:, lanes]
        sig = 1.0 / (1.0 + jnp.exp(-u))
        s["f"][block] = (u * sig).astype(BF16)
        s["slope"][block] = sig * (1.0 + u * (1.0 - sig))

    def ff_down(block):
        s["r3"][...] += mm_nt(s["f"][block], weight(REDUCE + block))

    def live_rows(each):
        row = lax.broadcasted_iota(jnp.int32, (rows, 1), 0)
        count = jnp.zeros((rows, 1), jnp.int32)
        for slot in range(slots):
            here_count = jnp.where(routes_ref[slot] >= 0, each(slot), 0)
            count = jnp.where((row >= slot * span) & (row < (slot + 1) * span), here_count + slot * span, count)
        return row < count

    def close():
        unit, rstd = normed(s["r3"][...])
        y = unit * bias(8) + bias(11)
        y = jnp.where(live_rows(lambda slot: span), y, 0.0)
        out_ref[...] = y.astype(BF16).reshape(out_ref.shape)
        dy = dy_ref[...].reshape(rows, width).astype(F32)
        dy = jnp.where(live_rows(lambda slot: lengths_ref[slot]), dy, 0.0)
        dr3 = norm_back(dy, unit, rstd, 2)
        s["dr"][...] = dr3
        s["e"][...] = dr3.astype(BF16)
        s["rows_grad"][12:13, :] = column_sum(s["e"][...])

    def reduce_grad(block):
        put_grad(REDUCE + block, mm_tn(s["e"][...], s["f"][block]))

    def ff_back(block):
        lanes = slice(block * width, (block + 1) * width)
        du = (mm(s["e"][...], weight(REDUCE + block)) * s["slope"][block]).astype(BF16)
        s["ebias_grad"][:, lanes] = column_sum(du)
        put_grad(EXPAND + block, mm_tn(s["h2b"][...], du))
        s["dr"][...] += mm_nt(du, weight(EXPAND + block))

    def cross_open():
        dr2 = norm_back(s["dr"][...], s["n2"][...], s["d2"][...], 1)
        s["dr"][...] = dr2
        e2 = dr2.astype(BF16)
        s["rows_grad"][5:6, :] = column_sum(e2)
        put_grad(CO, mm_tn(s["a2"][...], e2))
        s["da"][...] = mm_nt(e2, weight(CO)).astype(BF16)

    def score_grad(low, grads):
        weights = low.astype(F32)
        return (weights * (grads - jnp.sum(weights * grads, axis=-1, keepdims=True))).astype(BF16)

    def cross_back(slot):
        at = slice(slot * span, (slot + 1) * span)

        def body(pair, carry):
            lanes = pl.ds(pl.multiple_of(pair * LANES, LANES), LANES)
            da = stack(s["da"][at, lanes])
            low = s["pc"][slot, pair]
            ds = score_grad(low, mm_nt(da, keys("v2", slot, lanes)))
            s["dq"][at, lanes] = unstack(mm(ds, keys("k2", slot, lanes)), scale).astype(BF16)
            shape = (members, chunk, LANES)
            s["dk2"][slot, :, :, lanes] = mm_tn(ds, stack(s["q2"][at, lanes], scale)).astype(BF16).reshape(shape)
            s["dv2"][slot, :, :, lanes] = mm_tn(low, da).astype(BF16).reshape(shape)
            return carry
        lax.fori_loop(0, pairs, body, 0)

    def memory_grad(slot):
        def body(part, carry):
            value = mm_nt(s["dk2"][slot, part], weight(CK)) + mm_nt(s["dv2"][slot, part], weight(CV))
            s["gmem"][slot, part] = value.astype(BF16)
            return carry
        lax.fori_loop(0, members, body, 0)

    def send_memory_grad(slot):
        mine = gmem_ref.at[place.mem * slots + slot]
        keep = pltpu.make_async_copy(s["gmem"].at[slot, place.mem], mine, s["local"].at[3 + slot])
        keep.start()
        local_waits.append(keep)
        for hop, other in zip(range(1, members), others):
            sender = lax.rem(place.mem + members - hop, members)
            grad_waits.append(
                links.copy(
                    s["gmem"].at[slot, other], mine, gmem_ref.at[sender * slots + slot], (place.bucket, other)
                )
            )

    local_waits, grad_waits = [], []

    def cross_query_grad():
        dq = s["dq"][...]
        s["rows_grad"][3:4, :] = column_sum(dq)
        put_grad(CQ, mm_tn(s["h1b"][...], dq))

    def memory_weight_grad():
        for name, number in (("dk2", CK), ("dv2", CV)):
            s["acc"][...] = jnp.zeros_like(s["acc"])

            def body(part, carry, name=name):
                for slot in range(slots):
                    s["acc"][...] += mm_tn(s["mem"][slot, part], s[name][slot, part])
                return carry
            lax.fori_loop(0, members, body, 0)
            put_grad(number, s["acc"][...])
        total = jnp.zeros((1, width), F32)
        for slot in range(slots):
            for part in range(members):
                total += column_sum(s["dv2"][slot, part])
        s["rows_grad"][4:5, :] = total

    def self_open():
        dh1 = s["dr"][...] + mm_nt(s["dq"][...], weight(CQ))
        dr1 = norm_back(dh1, s["n1"][...], s["d1"][...], 0)
        s["dr"][...] = dr1
        e1 = dr1.astype(BF16)
        s["rows_grad"][2:3, :] = column_sum(e1)
        put_grad(SO, mm_tn(s["a"][...], e1))
        s["da"][...] = mm_nt(e1, weight(SO)).astype(BF16)

    def self_back():
        for slot in range(slots):
            at = slice(slot * span, (slot + 1) * span)
            for pair in range(pairs):
                lanes = slice(pair * LANES, (pair + 1) * LANES)
                da = stack(s["da"][at, lanes])
                low = s["ps"][slot, pair]
                ds = score_grad(low, mm_nt(da, s["v"][at, lanes]))
                s["dq"][at, lanes] = unstack(mm(ds, s["k"][at, lanes]), scale).astype(BF16)
                s["dk"][at, lanes] = mm_tn(ds, stack(s["q"][at, lanes], scale)).astype(BF16)
                s["dv"][at, lanes] = mm_tn(low, da).astype(BF16)

    def self_grads():
        x = x_ref[...].reshape(rows, width)
        put_grad(SV, mm_tn(x, s["dv"][...]))
        put_grad(SQ, mm_tn(x, s["dq"][...]))
        put_grad(SK, mm_tn(x, s["dk"][...]))
        s["rows_grad"][0:1, :] = column_sum(s["dq"][...])
        s["rows_grad"][1:2, :] = column_sum(s["dv"][...])

    def input_grad():
        total = s["dr"][...] + mm_nt(s["dq"][...], weight(SQ))
        total += mm_nt(s["dk"][...], weight(SK)) + mm_nt(s["dv"][...], weight(SV))
        dx_ref[...] = total.astype(BF16).reshape(dx_ref.shape)

    def pack_small():
        places = width // ROWS
        group, share = LANES // ROWS, LANES // (width * ff_blocks // places)
        row = lax.broadcasted_iota(jnp.int32, (ROWS, LANES), 0)
        for first in range(0, places, share):
            g = first // group
            base = s["rows_grad"][:, g * LANES : (g + 1) * LANES]
            piece = first // share
            extra = s["ebias_grad"][:, piece * LANES : (piece + 1) * LANES]
            value = jnp.where(row == 13, extra, base).astype(BF16)
            for number in range(first, first + share):
                index, rest = [], number
                for axis in reversed(AXES):
                    index.insert(0, rest % grid[axis])
                    rest //= grid[axis]
                s["gsmall"][tuple(index)] = value

    def emit_weight(low, high):
        def emit(total):
            gw_ref[low:high] = total / s["tokens"][0:1, 0:1]
        return emit

    def emit_small(total):
        gs_ref[...] = total / s["tokens"][0:1, 0:1]

    scatters = []
    for number, (low, high, order) in enumerate(SCATTER_CHUNKS):
        parts, landings, emit = [(s["gw"], (slice(low, high),))], [s["land"][number]], [emit_weight(low, high)]
        if number == len(SCATTER_CHUNKS) - 1:
            parts.append((s["gsmall"], ()))
            landings.append(s["land_small"])
            emit.append(emit_small)
        scatters.append(Scatter(links, place, grid, order, parts, landings, emit))

    def advance(work, upto, depth):
        for number in range(min(upto, len(work) - 1), -1, -1):
            pass

    s["rows_grad"][...] = jnp.zeros_like(s["rows_grad"])
    for gather in gathers:
        gather.step()
    send_memory()
    steps = len(gathers[0].order) + 1

    def wave(work, time):
        for number in range(len(work)):
            if work[number].done == time - number and 1 <= work[number].done < steps:
                work[number].step()

    time = 1

    def until(number):
        nonlocal time
        while gathers[number].done < steps:
            wave(gathers, time)
            time += 1

    until(0)
    unpack_small()
    until(1)
    self_project()
    self_attend()
    until(2)
    own_memory.wait()
    for wait in memory_waits:
        wait.wait_recv()
    cross_memory(0)
    cross_memory(1)
    until(3)
    self_close()
    cross_query()
    cross_attend(0)
    until(4)
    cross_attend(1)
    cross_close()
    for block in range(2):
        ff_up(block)
    until(5)
    for block in range(2, 4):
        ff_up(block)
    until(6)
    for block in range(2):
        ff_down(block)
    until(7)
    for block in range(2, 4):
        ff_down(block)
    close()

    started = 0

    def launch():
        nonlocal started
        scatters[started].step()
        started += 1

    def tick():
        for number in range(started):
            if scatters[number].done < steps:
                scatters[number].step()

    reduce_grad(3)
    reduce_grad(2)
    launch()
    reduce_grad(1)
    reduce_grad(0)
    tick()
    launch()
    ff_back(3)
    ff_back(2)
    tick()
    launch()
    ff_back(1)
    ff_back(0)
    tick()
    launch()
    cross_open()
    cross_back(0)
    memory_grad(0)
    send_memory_grad(0)
    tick()
    cross_back(1)
    memory_grad(1)
    send_memory_grad(1)
    tick()
    cross_query_grad()
    launch()
    memory_weight_grad()
    tick()
    launch()
    self_open()
    self_back()
    self_grads()
    pack_small()
    tick()
    launch()
    launch()
    input_grad()
    while any(scatter.done < steps for scatter in scatters):
        tick()
    for wait in grad_waits:
        wait.wait_recv()
    for wait in local_waits:
        wait.wait()
    links.finish()


def copy_count(grid, members, slots):
    count = 0
    for index, (_, _, order) in enumerate(GATHER_CHUNKS):
        count += sum(grid[axis] - 1 for axis in order) * (2 if index == 0 else 1)
    for index, (_, _, order) in enumerate(SCATTER_CHUNKS):
        count += sum(grid[axis] - 1 for axis in order) * (2 if index == len(SCATTER_CHUNKS) - 1 else 1)
    return count + (members - 1) * (1 + slots)


def run_layer(sizes, grid, lengths, reaches, routes, x, dy, pack, small, memory):
    slots, span, width = x.shape
    rows = slots * span
    members = sizes["x"] * sizes["c"]
    chunk = memory.shape[1]
    pairs = width // HD // 2
    ff_blocks = (BLOCKS - EXPAND) // 2
    place = tuple(grid[axis] for axis in AXES)
    mem_shape = (slots, members, chunk, width)
    count = copy_count(grid, members, slots)
    scratch = {
        "w": pltpu.VMEM((BLOCKS,) + place + (ROWS, width), BF16),
        "small": pltpu.VMEM(place + (ROWS, LANES), BF16),
        "gw": pltpu.VMEM((BLOCKS,) + place + (ROWS, width), BF16),
        "gsmall": pltpu.VMEM(place + (ROWS, LANES), BF16),
        "land": [
            landing_shapes(grid, order, (high - low,), (ROWS, width)) for low, high, order in SCATTER_CHUNKS
        ],
        "land_small": landing_shapes(grid, SCATTER_CHUNKS[-1][2], (), (ROWS, LANES)),
        "pc": pltpu.VMEM((slots, pairs, 2 * span, members * chunk), BF16),
        "ps": pltpu.VMEM((slots, pairs, 2 * span, span), BF16),
        "f": pltpu.VMEM((ff_blocks, rows, width), BF16),
        "slope": pltpu.VMEM((ff_blocks, rows, width), F32),
        "rows": pltpu.VMEM((ROWS, width), F32),
        "rows_grad": pltpu.VMEM((ROWS, width), F32),
        "ebias": pltpu.VMEM((1, width * ff_blocks), F32),
        "ebias_grad": pltpu.VMEM((1, width * ff_blocks), F32),
        "tokens": pltpu.VMEM((8, LANES), F32),
        "acc": pltpu.VMEM((width, width), F32),
        "d1": pltpu.VMEM((rows, 1), F32),
        "d2": pltpu.VMEM((rows, 1), F32),
        "send": pltpu.SemaphoreType.DMA((count,)),
        "recv": pltpu.SemaphoreType.DMA((count,)),
        "local": pltpu.SemaphoreType.DMA((3 + slots,)),
    }
    for name in ("mem", "k2", "v2", "dk2", "dv2", "gmem"):
        scratch[name] = pltpu.VMEM(mem_shape, BF16)
    for name in ("q", "k", "v", "a", "h1b", "q2", "a2", "h2b", "e", "da", "dq", "dk", "dv"):
        scratch[name] = pltpu.VMEM((rows, width), BF16)
    for name in ("n1", "n2", "h1", "r3", "dr"):
        scratch[name] = pltpu.VMEM((rows, width), F32)
    leaves, tree = jax.tree.flatten(scratch)

    def kernel(*refs):
        fixed = refs[: len(refs) - len(leaves)]
        layer_kernel(sizes, grid, *fixed, jax.tree.unflatten(tree, refs[len(fixed) :]))

    vmem, smem = pl.BlockSpec(memory_space=pltpu.VMEM), pl.BlockSpec(memory_space=pltpu.SMEM)
    anywhere = pl.BlockSpec(memory_space=pl.ANY)
    return pl.pallas_call(
        kernel,
        out_shape=(
            jax.ShapeDtypeStruct(x.shape, BF16),
            jax.ShapeDtypeStruct(x.shape, BF16),
            jax.ShapeDtypeStruct(pack.shape, F32),
            jax.ShapeDtypeStruct(small.shape, F32),
            jax.ShapeDtypeStruct(memory.shape, BF16),
        ),
        in_specs=[smem] * 3 + [vmem] * 2 + [anywhere] * 3,
        out_specs=[vmem] * 4 + [anywhere],
        scratch_shapes=leaves,
        compiler_params=pltpu.CompilerParams(
            collective_id=0, has_side_effects=True, vmem_limit_bytes=62 << 20
        ),
    )(lengths, reaches, routes, x, dy, pack, small, memory)


def shards(
    sizes,
    decoder_in, memory, grad_out, decoder_lengths, memory_lengths, item_route,
    in_projection, out_projection, attention_bias, expand_weight, expand_bias,
    reduce_weight, reduce_bias, norm_gain, norm_bias,
):
    own_rows, width = in_projection.shape[1:]
    ff = expand_weight.shape[1] // width

    def cut(weight):
        return weight.reshape(own_rows, ff, width).transpose(1, 0, 2)

    pack = jnp.concatenate(
        [
            in_projection[0:3], out_projection[0:1], in_projection[4:6], in_projection[3:4],
            out_projection[1:2], cut(expand_weight), cut(reduce_weight.T),
        ],
        axis=0,
    )
    narrow = jnp.concatenate([attention_bias, norm_gain, norm_bias, reduce_bias[None]], axis=0)
    live = jnp.where(item_route >= 0, decoder_lengths, 0).astype(BF16)
    joined = own_rows < ROWS
    bucket, mem = lax.axis_index("bucket"), lax.axis_index("mem")
    if joined:
        pack = lax.all_gather(pack, "mem", axis=1, tiled=True)
        narrow = lax.all_gather(narrow, "mem", axis=1, tiled=True)
        expand_bias = lax.all_gather(expand_bias, "mem", axis=0, tiled=True)
        live = lax.all_gather(live, "mem", axis=0, tiled=True)
        grid = dict(sizes, x=1, c=1)
        spot = bucket
    else:
        grid = dict(sizes)
        spot = bucket * (sizes["x"] * sizes["c"]) + mem
    lane = jnp.arange(LANES)

    def spread(values):
        size = values.shape[-1]
        tiled = jnp.tile(values, (1, LANES // size))
        return jnp.where(lane // size == spot % (LANES // size), tiled, jnp.zeros_like(tiled))

    small = jnp.concatenate(
        [
            spread(narrow), spread(expand_bias[None]),
            jnp.pad(live[None], ((0, 2), (0, LANES - live.shape[0])))[:2],
        ],
        axis=0,
    )
    small = jnp.pad(small, ((0, ROWS - small.shape[0]), (0, 0)))
    decoder_out, grad_decoder, grad_blocks, grad_small, grad_memory = run_layer(
        sizes, grid, decoder_lengths, memory_lengths, item_route, decoder_in, grad_out, pack, small, memory
    )

    def picked(values, size):
        return lax.dynamic_slice_in_dim(values, (spot % (LANES // size)) * size, size, axis=1)

    grad_narrow = picked(grad_small[0:13], ROWS)
    grad_ebias = picked(grad_small[13:14], expand_bias.shape[0])[0]
    if joined:
        grad_blocks = lax.psum_scatter(grad_blocks, "mem", scatter_dimension=1, tiled=True)
        grad_narrow = lax.psum_scatter(grad_narrow, "mem", scatter_dimension=1, tiled=True)
        grad_ebias = lax.psum_scatter(grad_ebias, "mem", scatter_dimension=0, tiled=True)

    def joined_back(blocks):
        return blocks.transpose(1, 0, 2).reshape(own_rows, ff * width)

    g = grad_blocks
    return (
        decoder_out,
        grad_decoder,
        grad_memory,
        jnp.concatenate([g[0:3], g[CQ : CQ + 1], g[CK : CV + 1]], axis=0),
        jnp.concatenate([g[SO : SO + 1], g[CO : CO + 1]], axis=0),
        grad_narrow[0:6],
        joined_back(g[EXPAND:REDUCE]),
        grad_ebias,
        joined_back(g[REDUCE:BLOCKS]).T,
        grad_narrow[12],
        grad_narrow[6:9],
        grad_narrow[9:12],
    )


def solution(mesh):
    both = ("bucket", "mem")
    buckets, members = mesh.shape["bucket"], mesh.shape["mem"]
    cores = 2
    across = members // cores
    sizes = {"z": buckets // across, "y": across, "x": across, "c": cores}
    in_specs = (
        P(both, None, None), P("bucket", "mem", None), P(both, None, None), P(both), P(both), P(both),
        P(None, both, None), P(None, both, None), P(None, both), P(both, None), P(both),
        P(None, both), P(both), P(None, both), P(None, both),
    )
    out_specs = (
        P(both, None, None), P(both, None, None), P("bucket", "mem", None),
        P(None, both, None), P(None, both, None), P(None, both), P(both, None), P(both),
        P(None, both), P(both), P(None, both), P(None, both),
    )
    return jax.shard_map(
        functools.partial(shards, sizes), mesh=mesh, in_specs=in_specs, out_specs=out_specs, check_vma=False
    )
```

time: 1230 us -> 200 us (0.16)
  waiting for transfers between devices: 827 us -> 0 us
  blocking collectives: 206 us -> 0 us
  Pallas kernels: 0 us -> 174 us
  matrix products: 66.2 us -> 0 us
  other arithmetic: 41.5 us -> 3.38 us
  starting transfers between devices: 34.5 us -> 0 us
  between operations: 27.2 us -> 0.74 us
    reduce_scatter x4 -> x0, waiting for transfers between devices: 521 us -> none  [the longest x1 140 us: shards(): lax.psum_scatter(grad_expand, ('bucket', 'mem'), scatter_dimension=0, til...]
    unnamed x14 -> x0, waiting for transfers between devices: 263 us -> none
    pallas_call x0 -> x1, Pallas kernels: none -> 174 us  [run_layer(): pl.pallas_call(kernel, out_shape=(jax.ShapeDtypeStruct(x.shape, BF16), ja...]
    all_gather x3 -> x0, blocking collectives: 113 us -> none  [the longest x1 38.6 us: shards(): lax.all_gather(attention_bias, ('bucket', 'mem'), axis=1, tiled=True)]
    dot_general x42 -> x0, matrix products: 66.2 us -> none  [the longest x10 19.9 us: weight_grad(): jnp.einsum('rd,re->de', rows_in, grad_rows, preferred_element_type=jnp.fl...]
    psum x1 -> x0, blocking collectives: 55.1 us -> none  [shards(): lax.psum(jnp.sum(length_work.astype(jnp.float32)), ('bucket', 'mem'))]
    ppermute x8 -> x0, waiting for transfers between devices: 42.5 us -> none  [shifted(): lax.ppermute(value, axis, [(source, source + steps) for source in range(f...]
    unnamed x1 -> x0, blocking collectives: 37.2 us -> none
  transfers between devices with their start and end apart: 21 -> 0, of which waited for: 9 -> 0; matrix products, arithmetic and copies ran while one was open for 7% -> 0% of each run, Pallas kernels for 0% -> 0%
where the time goes in v1:
time: 200 us; the launch traced here: 199 us
  Pallas kernels  174 us (87%)
  local copies, waits for them, and re-layouts  21 us (10%)
  other arithmetic  3.38 us (2%)
    pallas_call x1, Pallas kernels, run_layer(): pl.pallas_call(kernel, out_shape=(jax.ShapeDtypeStruct(x.shape, BF16), ja...  174 us
    unnamed x16, local copies, waits for them, and re-layouts  9.95 us

profile of v1, /device:TPU:0, one launch (start us, length us, event | category | flops | bytes accessed | tf_op | source)
XLA Modules:
  0.0 199.3 jit_solution(6581925588207448760)
XLA Ops:
  0.7 0.7 tile.19
  1.3 0.1 tile.20
  1.4 0.7 fusion.4
  2.1 0.7 pad_maximum_fusion.2
  2.9 0.1 tile.18
  3.0 0.6 pad_maximum_fusion.3.refs_6_
  3.6 0.8 slice_dynamic-update-slice_fusion
  4.4 0.7 constant_dynamic-update-slice_fusion.2
  5.1 0.8 slice_dynamic-update-slice_fusion.1
  5.9 0.7 constant_dynamic-update-slice_fusion.1
  6.6 0.7 constant_dynamic-update-slice_fusion
  7.3 0.8 fusion.1
  8.2 0.8 fusion.refs_5_
  9.0 0.0 copy-start.1
  9.0 0.7 copy-done.1
  9.7 174.2 %shard_map.238 = (bf16[2,128,512]{2,1,0:T(8,128)(2,1)}, bf16[2,128,512]{2,1,0:T(8,128)(2,1)}, f32[16,16,512]{2,1,0:T(8,128)}, f32[16,128]{1,0:T(8,128)}, bf16[8,256,512]{2,1,0:T(8,128)(2,1)}) custom-call(s32[2]{0:T(128)} %refs_0_.1, s32[2]{0:T(128)} %refs_1_.1, s32[2]{0:T(128)} %refs_2_.1, bf16[2,128,512]{2,1,0:T(8,128)(2,1)} %refs_3_.1, ...), custom_call_target="tpu_custom_call" | custom-call | tf_op jit(solution)/shard_map/pallas_call | solution.py:707
  184.0 0.0 copy-start.2
  184.0 0.0 copy-start
  184.0 1.4 dynamic-slice_bitcast_fusion
  185.4 0.7 slice.71
  186.1 0.6 dynamic-slice_bitcast_fusion.1
  186.7 1.4 fusion.6
  188.1 1.3 constant_dynamic-slice_fusion
  189.4 0.8 slice.65
  190.3 0.9 slice.63
  191.2 0.8 fusion.5
  192.0 1.0 slice_bitcast_fusion
  193.0 0.7 copy.34
  193.6 0.6 pad_maximum_fusion.1
  194.3 0.7 pad_maximum_fusion
  194.9 0.7 copy.33
  195.6 1.7 copy.46
  197.3 0.0 copy-done.2
  197.3 0.7 copy.47
  198.0 0.0 copy-done
  198.0 1.3 copy.48
  (5 shorter events, 0.0 us)
Async XLA Ops:
  9.0 0.7 copy-start.1
  184.0 13.3 %copy-start.2 = (bf16[2,128,512]{2,1,0:T(8,128)(2,1)S(1)}, bf16[2,128,512]{2,1,0:T(8,128)(2,1)}, u32[]{:S(2)}) copy-start(bf16[2,128,512]{2,1,0:T(8,128)(2,1)} %get-tuple-element.42) | copy-start | bytes 786436
  184.0 14.0 %copy-start = (bf16[8,256,512]{2,1,0:T(8,128)(2,1)S(1)}, bf16[8,256,512]{2,1,0:T(8,128)(2,1)}, u32[]{:S(2)}) copy-start(bf16[8,256,512]{2,1,0:T(8,128)(2,1)} %get-tuple-element.43) | copy-start | bytes 6291460

commit v2 on v1

--- a/solution.py
+++ b/solution.py
@@ -18,8 +18,14 @@
 
 SQ, SK, SV, SO, CK, CV, CQ, CO, EXPAND, REDUCE = 0, 1, 2, 3, 4, 5, 6, 7, 8, 12
 BLOCKS = 16
-GATHER_CHUNKS = tuple((low, low + 2, "zxyc") for low in range(0, BLOCKS, 2))
-SCATTER_CHUNKS = tuple((low, low + 2, "cyxz") for low in range(BLOCKS - 2, -1, -2))
+GATHER_CHUNKS = (
+    (0, 2, "xzyc"), (2, 4, "xzyc"), (4, 6, "zyxc"), (6, 8, "xzyc"),
+    (8, 10, "xzyc"), (10, 12, "xzyc"), (12, 14, "zyxc"), (14, 16, "xyzc"),
+)
+SCATTER_CHUNKS = (
+    (14, 16, "cyzx"), (12, 14, "cyzx"), (10, 12, "czyx"), (8, 10, "cyzx"),
+    (6, 8, "cyzx"), (4, 6, "cyzx"), (2, 4, "cxzy"), (0, 2, "cyxz"),
+)
 AXES = "zyxc"
 
 
@@ -91,7 +97,13 @@
         self.order = [axis for axis in order if grid[axis] > 1]
         self.grid, self.waits, self.done = grid, [], 0
 
+    @property
+    def over(self):
+        return self.done > len(self.order)
+
     def step(self):
+        if self.over:
+            return
         for wait in self.waits:
             wait.wait_recv()
         self.waits = []
@@ -130,7 +142,13 @@
             for axis in AXES
         }
 
+    @property
+    def over(self):
+        return self.done > len(self.order)
+
     def step(self):
+        if self.over:
+            return
         for wait in self.waits:
             wait.wait_recv()
         self.waits = []
@@ -140,9 +158,13 @@
             index = self.index(self.order[: self.done])
             for number, (ref, lead) in enumerate(self.parts):
                 where = tuple(lead) + tuple(index[name] for name in AXES)
+                landed = self.landings[number][self.done - 1]
+                if self.grid[axis] == 2 and not last:
+                    ref[where] = ref[where] + landed[0]
+                    continue
                 total = ref[where].astype(F32)
                 for hop in range(1, self.grid[axis]):
-                    total += self.landings[number][self.done - 1][hop - 1].astype(F32)
+                    total += landed[hop - 1].astype(F32)
                 if last:
                     self.emit[number](total)
                 else:
@@ -176,13 +198,17 @@
 
 def layer_kernel(
     sizes, grid,
-    lengths_ref, reaches_ref, routes_ref, x_ref, dy_ref, pack_ref, small_ref, memory_ref,
-    out_ref, dx_ref, gw_ref, gs_ref, gmem_ref,
+    lengths_ref, reaches_ref, routes_ref, all_lengths_ref, all_routes_ref,
+    attention_bias_ref, gain_ref, shift_ref, reduce_bias_ref, expand_bias_ref,
+    x_hbm, dy_hbm, in_hbm, out_hbm, expand_hbm, reduce_hbm, memory_ref,
+    grad_bias_ref, grad_gain_ref, grad_shift_ref, grad_reduce_bias_ref, grad_expand_bias_ref,
+    y_hbm, dx_hbm, grad_in_hbm, grad_out_hbm, grad_expand_hbm, grad_reduce_hbm, gmem_ref,
     scratch,
 ):
     s = scratch
     place = Place(sizes)
     links = Links(s["send"], s["recv"])
+    x_ref, dy_ref = s["x"], s["dy"]
     slots, span, width = x_ref.shape
     rows = slots * span
     members, chunk = s["mem"].shape[1], s["mem"].shape[2]
@@ -190,6 +216,14 @@
     heads = width // HD
     pairs = heads // 2
     ff_blocks = (BLOCKS - EXPAND) // 2
+    places = width // ROWS
+    locals_used = [0]
+
+    def local_copy(source, target):
+        locals_used[0] += 1
+        copy = pltpu.make_async_copy(source, target, s["local"].at[locals_used[0] - 1])
+        copy.start()
+        return copy
 
     barrier = pltpu.get_barrier_semaphore()
     peers = []
@@ -200,19 +234,45 @@
     for peer in peers:
         pl.semaphore_signal(barrier, inc=1, device_id=peer, device_id_type=MESH)
 
-    def here(ref, lead=()):
-        return block_view(ref, lead, {a: place.at[a] if grid[a] > 1 else 0 for a in AXES})
+    here = tuple(place.at[axis] if grid[axis] > 1 else 0 for axis in AXES)
+
+    def block_parts(in_ref, out_ref, expand_ref, reduce_ref):
+        parts = [(SQ + k, in_ref.at[k]) for k in range(3)] + [(CQ, in_ref.at[3]), (CK, in_ref.at[4])]
+        parts += [(CV, in_ref.at[5]), (SO, out_ref.at[0]), (CO, out_ref.at[1])]
+        for k in range(ff_blocks):
+            lanes = pl.ds(k * width, width)
+            parts += [(EXPAND + k, expand_ref.at[:, lanes]), (REDUCE + k, reduce_ref.at[:, lanes])]
+        return sorted(parts, key=lambda part: part[0])
 
     own = [
-        pltpu.make_async_copy(pack_ref, here(s["w"], (slice(None),)), s["local"].at[0]),
-        pltpu.make_async_copy(small_ref, here(s["small"]), s["local"].at[1]),
+        local_copy(part, s["w"].at[(number,) + here])
+        for number, part in block_parts(in_hbm, out_hbm, expand_hbm, reduce_hbm)
     ]
-    own_memory = pltpu.make_async_copy(
-        memory_ref.at[pl.ds(place.mem * slots, slots)], s["mem"].at[:, place.mem], s["local"].at[2]
-    )
-    for copy in own:
-        copy.start()
-    own_memory.start()
+    own_rows = [local_copy(x_hbm, x_ref), local_copy(dy_hbm, dy_ref)]
+    own_memory = local_copy(memory_ref.at[pl.ds(place.mem * slots, slots)], s["mem"].at[:, place.mem])
+
+    spot = here[0]
+    for axis, at in zip(AXES[1:], here[1:]):
+        spot = spot * grid[axis] + at
+    share = expand_bias_ref.shape[1]
+    group, pieces = LANES // ROWS, LANES // share
+    packet = s["packet"]
+    packet[...] = jnp.zeros_like(packet)
+    packet[0:6, 0:ROWS] = attention_bias_ref[...].astype(F32)
+    packet[6:9, 0:ROWS] = gain_ref[...].astype(F32)
+    packet[9:12, 0:ROWS] = shift_ref[...].astype(F32)
+    packet[12:13, 0:ROWS] = reduce_bias_ref[...].astype(F32)
+    packet[13:14, 0:share] = expand_bias_ref[...].astype(F32)
+    narrow = pltpu.roll(packet[...], lax.rem(spot, group) * ROWS, 1)
+    wide = pltpu.roll(packet[...], lax.rem(spot, pieces) * share, 1)
+    row = lax.broadcasted_iota(jnp.int32, (ROWS, LANES), 0)
+    lane = lax.broadcasted_iota(jnp.int32, (ROWS, LANES), 1)
+    live = jnp.zeros((ROWS, LANES), jnp.int32)
+    for slot in range(all_lengths_ref.shape[0]):
+        count = jnp.where(all_routes_ref[slot] >= 0, all_lengths_ref[slot], 0)
+        live = jnp.where(lane == slot, count, live)
+    value = jnp.where(row == 13, wide, jnp.where(row == 14, live.astype(F32), narrow))
+    s["small"][here] = value.astype(BF16)
     for copy in own:
         copy.wait()
     pl.semaphore_wait(barrier, len(peers))
@@ -223,15 +283,17 @@
         if number == 0:
             parts.append((s["small"], ()))
         gathers.append(Gather(links, place, grid, order, parts))
-    memory_waits = []
-
-    def send_memory():
+    memory_waits = [[] for _ in range(slots)]
+    half = chunk // 2
+
+    def send_memory(slot, part):
+        at = pl.ds(part * half, half)
         for hop, other in zip(range(1, members), others):
             sender = lax.rem(place.mem + members - hop, members)
-            memory_waits.append(
+            memory_waits[slot].append(
                 links.copy(
-                    memory_ref.at[pl.ds(other * slots, slots)], s["mem"].at[:, place.mem],
-                    s["mem"].at[:, sender], (place.bucket, other),
+                    memory_ref.at[other * slots + slot, at], s["mem"].at[slot, place.mem, at],
+                    s["mem"].at[slot, sender, at], (place.bucket, other),
                 )
             )
 
@@ -242,8 +304,8 @@
         ref = s["gw"]
         ref[number] = value.astype(BF16).reshape(ref.shape[1:])
 
-    lane = lax.broadcasted_iota(jnp.int32, (1, LANES), 1)
-    even = jnp.where(lane < HD, 1.0, 0.0)
+    even_lanes = lax.broadcasted_iota(jnp.int32, (1, LANES), 1) < HD
+    even = jnp.where(even_lanes, 1.0, 0.0)
     odd = 1.0 - even
     scale = HD ** (-0.5)
 
@@ -274,16 +336,13 @@
         return s["rows"][number : number + 1, :]
 
     def unpack_small():
-        places = width // ROWS
         every = s["small"][...].reshape(places, ROWS, LANES).astype(F32)
-        group = LANES // ROWS
         columns = [jnp.sum(every[g * group : (g + 1) * group], axis=0) for g in range(places // group)]
         s["rows"][...] = jnp.concatenate(columns, axis=1)
-        share = LANES // (width * ff_blocks // places)
-        pieces = [
-            jnp.sum(every[g * share : (g + 1) * share, 13], axis=0, keepdims=True) for g in range(places // share)
+        columns = [
+            jnp.sum(every[g * pieces : (g + 1) * pieces, 13], axis=0, keepdims=True) for g in range(places // pieces)
         ]
-        s["ebias"][...] = jnp.concatenate(pieces, axis=1)
+        s["ebias"][...] = jnp.concatenate(columns, axis=1)
         tokens = jnp.sum(jnp.sum(every[:, 14], axis=0, keepdims=True), axis=1, keepdims=True)
         s["tokens"][...] = jnp.broadcast_to(tokens, s["tokens"].shape)
 
@@ -378,7 +437,8 @@
         unit, rstd = normed(s["r3"][...])
         y = unit * bias(8) + bias(11)
         y = jnp.where(live_rows(lambda slot: span), y, 0.0)
-        out_ref[...] = y.astype(BF16).reshape(out_ref.shape)
+        s["y"][...] = y.astype(BF16).reshape(x_ref.shape)
+        local_waits.append(local_copy(s["y"], y_hbm))
         dy = dy_ref[...].reshape(rows, width).astype(F32)
         dy = jnp.where(live_rows(lambda slot: lengths_ref[slot]), dy, 0.0)
         dr3 = norm_back(dy, unit, rstd, 2)
@@ -432,9 +492,7 @@
 
     def send_memory_grad(slot):
         mine = gmem_ref.at[place.mem * slots + slot]
-        keep = pltpu.make_async_copy(s["gmem"].at[slot, place.mem], mine, s["local"].at[3 + slot])
-        keep.start()
-        local_waits.append(keep)
+        local_waits.append(local_copy(s["gmem"].at[slot, place.mem], mine))
         for hop, other in zip(range(1, members), others):
             sender = lax.rem(place.mem + members - hop, members)
             grad_waits.append(
@@ -498,32 +556,41 @@
     def input_grad():
         total = s["dr"][...] + mm_nt(s["dq"][...], weight(SQ))
         total += mm_nt(s["dk"][...], weight(SK)) + mm_nt(s["dv"][...], weight(SV))
-        dx_ref[...] = total.astype(BF16).reshape(dx_ref.shape)
+        s["dx"][...] = total.astype(BF16).reshape(x_ref.shape)
+        local_waits.append(local_copy(s["dx"], dx_hbm))
+
+    def turned(value, lanes):
+        return value if lanes == 0 else pltpu.roll(value, LANES - lanes, 1)
 
     def pack_small():
-        places = width // ROWS
-        group, share = LANES // ROWS, LANES // (width * ff_blocks // places)
         row = lax.broadcasted_iota(jnp.int32, (ROWS, LANES), 0)
-        for first in range(0, places, share):
-            g = first // group
-            base = s["rows_grad"][:, g * LANES : (g + 1) * LANES]
-            piece = first // share
-            extra = s["ebias_grad"][:, piece * LANES : (piece + 1) * LANES]
-            value = jnp.where(row == 13, extra, base).astype(BF16)
-            for number in range(first, first + share):
-                index, rest = [], number
-                for axis in reversed(AXES):
-                    index.insert(0, rest % grid[axis])
-                    rest //= grid[axis]
-                s["gsmall"][tuple(index)] = value
+        for number in range(places):
+            at = number // group * LANES
+            base = turned(s["rows_grad"][:, at : at + LANES], number % group * ROWS)
+            at = number // pieces * LANES
+            extra = turned(s["ebias_grad"][:, at : at + LANES], number % pieces * share)
+            index, rest = [], number
+            for axis in reversed(AXES):
+                index.insert(0, rest % grid[axis])
+                rest //= grid[axis]
+            s["gsmall"][tuple(index)] = jnp.where(row == 13, extra, base).astype(BF16)
+
+    targets = dict(block_parts(grad_in_hbm, grad_out_hbm, grad_expand_hbm, grad_reduce_hbm))
 
     def emit_weight(low, high):
         def emit(total):
-            gw_ref[low:high] = total / s["tokens"][0:1, 0:1]
+            s["stage"][low:high] = total / s["tokens"][0:1, 0:1]
+            for number in range(low, high):
+                local_waits.append(local_copy(s["stage"].at[number], targets[number]))
         return emit
 
     def emit_small(total):
-        gs_ref[...] = total / s["tokens"][0:1, 0:1]
+        value = total / s["tokens"][0:1, 0:1]
+        grad_bias_ref[...] = value[0:6, 0:ROWS]
+        grad_gain_ref[...] = value[6:9, 0:ROWS]
+        grad_shift_ref[...] = value[9:12, 0:ROWS]
+        grad_reduce_bias_ref[...] = value[12:13, 0:ROWS]
+        grad_expand_bias_ref[...] = value[13:14, 0:share]
 
     scatters = []
     for number, (low, high, order) in enumerate(SCATTER_CHUNKS):
@@ -534,111 +601,116 @@
             emit.append(emit_small)
         scatters.append(Scatter(links, place, grid, order, parts, landings, emit))
 
-    def advance(work, upto, depth):
-        for number in range(min(upto, len(work) - 1), -1, -1):
-            pass
+    def gather(*numbers):
+        for number in numbers:
+            gathers[number].step()
+
+    def need(*numbers):
+        for number in numbers:
+            while not gathers[number].over:
+                gathers[number].step()
+
+    def scatter(*numbers):
+        for number in numbers:
+            scatters[number].step()
+
+    def arrived(copies):
+        for copy in copies:
+            copy.wait()
+
+    def arrived_memory(slot):
+        for wait in memory_waits[slot]:
+            wait.wait_recv()
 
     s["rows_grad"][...] = jnp.zeros_like(s["rows_grad"])
-    for gather in gathers:
-        gather.step()
-    send_memory()
-    steps = len(gathers[0].order) + 1
-
-    def wave(work, time):
-        for number in range(len(work)):
-            if work[number].done == time - number and 1 <= work[number].done < steps:
-                work[number].step()
-
-    time = 1
-
-    def until(number):
-        nonlocal time
-        while gathers[number].done < steps:
-            wave(gathers, time)
-            time += 1
-
-    until(0)
+    gather(0, 1, 2, 3, 4, 5, 6, 7)
+    send_memory(0, 0)
+    gather(0, 1, 3, 4, 2, 5, 7)
+    send_memory(0, 1)
+    gather(6, 2, 7, 0, 6, 1, 0, 2)
+    send_memory(1, 0)
+    gather(0)
+    need(0)
     unpack_small()
-    until(1)
+    gather(3, 2, 1, 6)
+    send_memory(1, 1)
+    gather(1)
+    need(1)
+    arrived(own_rows)
     self_project()
+    gather(4)
     self_attend()
-    until(2)
-    own_memory.wait()
-    for wait in memory_waits:
-        wait.wait_recv()
+    gather(3, 6)
+    self_close()
+    need(2)
+    arrived([own_memory])
+    arrived_memory(0)
     cross_memory(0)
-    cross_memory(1)
-    until(3)
-    self_close()
+    gather(5, 3)
+    need(3)
     cross_query()
     cross_attend(0)
-    until(4)
+    gather(4)
+    arrived_memory(1)
+    cross_memory(1)
     cross_attend(1)
+    gather(5, 4)
     cross_close()
-    for block in range(2):
-        ff_up(block)
-    until(5)
-    for block in range(2, 4):
-        ff_up(block)
-    until(6)
-    for block in range(2):
-        ff_down(block)
-    until(7)
-    for block in range(2, 4):
-        ff_down(block)
+    need(4)
+    ff_up(0)
+    gather(7)
+    ff_up(1)
+    gather(5)
+    need(5)
+    ff_up(2)
+    ff_up(3)
+    need(6)
+    ff_down(0)
+    ff_down(1)
+    gather(7)
+    need(7)
+    ff_down(2)
+    ff_down(3)
     close()
-
-    started = 0
-
-    def launch():
-        nonlocal started
-        scatters[started].step()
-        started += 1
-
-    def tick():
-        for number in range(started):
-            if scatters[number].done < steps:
-                scatters[number].step()
-
     reduce_grad(3)
     reduce_grad(2)
-    launch()
+    scatter(0)
     reduce_grad(1)
     reduce_grad(0)
-    tick()
-    launch()
+    scatter(1)
     ff_back(3)
     ff_back(2)
-    tick()
-    launch()
+    scatter(2)
     ff_back(1)
     ff_back(0)
-    tick()
-    launch()
+    scatter(0, 3, 1)
     cross_open()
+    scatter(2)
     cross_back(0)
+    scatter(3)
     memory_grad(0)
     send_memory_grad(0)
-    tick()
+    scatter(0)
     cross_back(1)
+    scatter(1)
     memory_grad(1)
     send_memory_grad(1)
-    tick()
+    scatter(2)
     cross_query_grad()
-    launch()
+    scatter(4)
     memory_weight_grad()
-    tick()
-    launch()
+    scatter(4, 5, 3, 0, 2)
     self_open()
     self_back()
+    scatter(5, 1)
     self_grads()
     pack_small()
-    tick()
-    launch()
-    launch()
+    scatter(6, 4, 7)
     input_grad()
-    while any(scatter.done < steps for scatter in scatters):
-        tick()
+    scatter(3, 6, 7, 0, 2, 1, 5, 3, 4, 6, 7, 4, 5, 7, 5, 6, 7, 6)
+    for work in scatters:
+        while not work.over:
+            work.step()
     for wait in grad_waits:
         wait.wait_recv()
     for wait in local_waits:
@@ -652,10 +724,11 @@
         count += sum(grid[axis] - 1 for axis in order) * (2 if index == 0 else 1)
     for index, (_, _, order) in enumerate(SCATTER_CHUNKS):
         count += sum(grid[axis] - 1 for axis in order) * (2 if index == len(SCATTER_CHUNKS) - 1 else 1)
-    return count + (members - 1) * (1 + slots)
-
-
-def run_layer(sizes, grid, lengths, reaches, routes, x, dy, pack, small, memory):
+    return count + (members - 1) * (2 * slots + slots)
+
+
+def run_layer(sizes, grid, scalars, small, large):
+    x, memory = large[0], large[-1]
     slots, span, width = x.shape
     rows = slots * span
     members = sizes["x"] * sizes["c"]
@@ -668,8 +741,10 @@
     scratch = {
         "w": pltpu.VMEM((BLOCKS,) + place + (ROWS, width), BF16),
         "small": pltpu.VMEM(place + (ROWS, LANES), BF16),
+        "packet": pltpu.VMEM((ROWS, LANES), F32),
         "gw": pltpu.VMEM((BLOCKS,) + place + (ROWS, width), BF16),
         "gsmall": pltpu.VMEM(place + (ROWS, LANES), BF16),
+        "stage": pltpu.VMEM((BLOCKS, ROWS, width), F32),
         "land": [
             landing_shapes(grid, order, (high - low,), (ROWS, width)) for low, high, order in SCATTER_CHUNKS
         ],
@@ -688,7 +763,7 @@
         "d2": pltpu.VMEM((rows, 1), F32),
         "send": pltpu.SemaphoreType.DMA((count,)),
         "recv": pltpu.SemaphoreType.DMA((count,)),
-        "local": pltpu.SemaphoreType.DMA((3 + slots,)),
+        "local": pltpu.SemaphoreType.DMA((2 * BLOCKS + 5 + slots,)),
     }
     for name in ("mem", "k2", "v2", "dk2", "dv2", "gmem"):
         scratch[name] = pltpu.VMEM(mem_shape, BF16)
@@ -696,6 +771,8 @@
         scratch[name] = pltpu.VMEM((rows, width), BF16)
     for name in ("n1", "n2", "h1", "r3", "dr"):
         scratch[name] = pltpu.VMEM((rows, width), F32)
+    for name in ("x", "dy", "y", "dx"):
+        scratch[name] = pltpu.VMEM(x.shape, BF16)
     leaves, tree = jax.tree.flatten(scratch)
 
     def kernel(*refs):
@@ -704,22 +781,45 @@
 
     vmem, smem = pl.BlockSpec(memory_space=pltpu.VMEM), pl.BlockSpec(memory_space=pltpu.SMEM)
     anywhere = pl.BlockSpec(memory_space=pl.ANY)
+    outs = [(part.shape, F32) for part in small]
+    outs += [(x.shape, BF16), (x.shape, BF16)] + [(part.shape, F32) for part in large[2:6]] + [(memory.shape, BF16)]
     return pl.pallas_call(
         kernel,
-        out_shape=(
-            jax.ShapeDtypeStruct(x.shape, BF16),
-            jax.ShapeDtypeStruct(x.shape, BF16),
-            jax.ShapeDtypeStruct(pack.shape, F32),
-            jax.ShapeDtypeStruct(small.shape, F32),
-            jax.ShapeDtypeStruct(memory.shape, BF16),
-        ),
-        in_specs=[smem] * 3 + [vmem] * 2 + [anywhere] * 3,
-        out_specs=[vmem] * 4 + [anywhere],
+        out_shape=tuple(jax.ShapeDtypeStruct(shape, dtype) for shape, dtype in outs),
+        in_specs=[smem] * len(scalars) + [vmem] * len(small) + [anywhere] * len(large),
+        out_specs=[vmem] * len(small) + [anywhere] * len(large),
         scratch_shapes=leaves,
         compiler_params=pltpu.CompilerParams(
             collective_id=0, has_side_effects=True, vmem_limit_bytes=62 << 20
         ),
-    )(lengths, reaches, routes, x, dy, pack, small, memory)
+    )(*scalars, *small, *large)
+
+
+def copy_kernel(*refs):
+    count = (len(refs) - 1) // 3
+    sources, targets, held, sems = refs[:count], refs[count : 2 * count], refs[2 * count : -1], refs[-1]
+    inward = [pltpu.make_async_copy(sources[n], held[n], sems.at[0, n]) for n in range(count)]
+    outward = [pltpu.make_async_copy(held[n], targets[n], sems.at[1, n]) for n in range(count)]
+    for copy in inward:
+        copy.start()
+    for came, goes in zip(inward, outward):
+        came.wait()
+        goes.start()
+    for copy in outward:
+        copy.wait()
+
+
+def handed_out(results):
+    anywhere = pl.BlockSpec(memory_space=pl.ANY)
+    return pl.pallas_call(
+        copy_kernel,
+        out_shape=tuple(jax.ShapeDtypeStruct(part.shape, part.dtype) for part in results),
+        in_specs=[anywhere] * len(results),
+        out_specs=[anywhere] * len(results),
+        scratch_shapes=[pltpu.VMEM(part.shape, part.dtype) for part in results]
+        + [pltpu.SemaphoreType.DMA((2, len(results)))],
+        compiler_params=pltpu.CompilerParams(vmem_limit_bytes=62 << 20),
+    )(*results)
 
 
 def shards(
@@ -728,79 +828,33 @@
     in_projection, out_projection, attention_bias, expand_weight, expand_bias,
     reduce_weight, reduce_bias, norm_gain, norm_bias,
 ):
-    own_rows, width = in_projection.shape[1:]
-    ff = expand_weight.shape[1] // width
-
-    def cut(weight):
-        return weight.reshape(own_rows, ff, width).transpose(1, 0, 2)
-
-    pack = jnp.concatenate(
-        [
-            in_projection[0:3], out_projection[0:1], in_projection[4:6], in_projection[3:4],
-            out_projection[1:2], cut(expand_weight), cut(reduce_weight.T),
-        ],
-        axis=0,
+    joined = in_projection.shape[1] < ROWS
+    small = [attention_bias, norm_gain, norm_bias, reduce_bias[None], expand_bias[None]]
+    weights = [in_projection, out_projection, expand_weight, reduce_weight.T]
+    along = (1, 1, 0, 0)
+    lengths, routes = decoder_lengths, item_route
+    grid = dict(sizes)
+    if joined:
+        grid.update(x=1, c=1)
+        small = [lax.all_gather(part, "mem", axis=1, tiled=True) for part in small]
+        weights = [lax.all_gather(part, "mem", axis=axis, tiled=True) for part, axis in zip(weights, along)]
+        lengths = lax.all_gather(lengths, "mem", tiled=True)
+        routes = lax.all_gather(routes, "mem", tiled=True)
+    results = run_layer(
+        sizes, grid, (decoder_lengths, memory_lengths, item_route, lengths, routes), small,
+        [decoder_in, grad_out] + weights + [memory],
     )
-    narrow = jnp.concatenate([attention_bias, norm_gain, norm_bias, reduce_bias[None]], axis=0)
-    live = jnp.where(item_route >= 0, decoder_lengths, 0).astype(BF16)
-    joined = own_rows < ROWS
-    bucket, mem = lax.axis_index("bucket"), lax.axis_index("mem")
     if joined:
-        pack = lax.all_gather(pack, "mem", axis=1, tiled=True)
-        narrow = lax.all_gather(narrow, "mem", axis=1, tiled=True)
-        expand_bias = lax.all_gather(expand_bias, "mem", axis=0, tiled=True)
-        live = lax.all_gather(live, "mem", axis=0, tiled=True)
-        grid = dict(sizes, x=1, c=1)
-        spot = bucket
+        results = list(results)
+        for number in range(5):
+            results[number] = lax.psum_scatter(results[number], "mem", scatter_dimension=1, tiled=True)
+        for number, axis in zip(range(7, 11), along):
+            results[number] = lax.psum_scatter(results[number], "mem", scatter_dimension=axis, tiled=True)
     else:
-        grid = dict(sizes)
-        spot = bucket * (sizes["x"] * sizes["c"]) + mem
-    lane = jnp.arange(LANES)
-
-    def spread(values):
-        size = values.shape[-1]
-        tiled = jnp.tile(values, (1, LANES // size))
-        return jnp.where(lane // size == spot % (LANES // size), tiled, jnp.zeros_like(tiled))
-
-    small = jnp.concatenate(
-        [
-            spread(narrow), spread(expand_bias[None]),
-            jnp.pad(live[None], ((0, 2), (0, LANES - live.shape[0])))[:2],
-        ],
-        axis=0,
-    )
-    small = jnp.pad(small, ((0, ROWS - small.shape[0]), (0, 0)))
-    decoder_out, grad_decoder, grad_blocks, grad_small, grad_memory = run_layer(
-        sizes, grid, decoder_lengths, memory_lengths, item_route, decoder_in, grad_out, pack, small, memory
-    )
-
-    def picked(values, size):
-        return lax.dynamic_slice_in_dim(values, (spot % (LANES // size)) * size, size, axis=1)
-
-    grad_narrow = picked(grad_small[0:13], ROWS)
-    grad_ebias = picked(grad_small[13:14], expand_bias.shape[0])[0]
-    if joined:
-        grad_blocks = lax.psum_scatter(grad_blocks, "mem", scatter_dimension=1, tiled=True)
-        grad_narrow = lax.psum_scatter(grad_narrow, "mem", scatter_dimension=1, tiled=True)
-        grad_ebias = lax.psum_scatter(grad_ebias, "mem", scatter_dimension=0, tiled=True)
-
-    def joined_back(blocks):
-        return blocks.transpose(1, 0, 2).reshape(own_rows, ff * width)
-
-    g = grad_blocks
+        results = handed_out(results)
+    bias, gain, shift, reduce_shift, expand_shift, out, dx, g_in, g_out, g_expand, g_reduce, g_memory = results
     return (
-        decoder_out,
-        grad_decoder,
-        grad_memory,
-        jnp.concatenate([g[0:3], g[CQ : CQ + 1], g[CK : CV + 1]], axis=0),
-        jnp.concatenate([g[SO : SO + 1], g[CO : CO + 1]], axis=0),
-        grad_narrow[0:6],
-        joined_back(g[EXPAND:REDUCE]),
-        grad_ebias,
-        joined_back(g[REDUCE:BLOCKS]).T,
-        grad_narrow[12],
-        grad_narrow[6:9],
-        grad_narrow[9:12],
+        out, dx, g_memory, g_in, g_out, bias, g_expand, expand_shift[0], g_reduce.T, reduce_shift[0], gain, shift,
     )
 
 

time: 200 us -> 131 us (0.66)
  Pallas kernels: 174 us -> 130 us
  local copies, waits for them, and re-layouts: 21 us -> 0 us
  other arithmetic: 3.38 us -> 0 us
    pallas_call x1 -> x2, Pallas kernels: 174 us -> 130 us  [the longest x1 126 us: run_layer(): pl.pallas_call(kernel, out_shape=tuple((jax.ShapeDtypeStruct(shape, dtype...]
    unnamed x16 -> x0, local copies, waits for them, and re-layouts: 9.95 us -> none
    slice x7 -> x0, local copies, waits for them, and re-layouts: 5.99 us -> none  [the longest x1 1.43 us: shards(): grad_narrow[9:12]]
    concatenate x4 -> x0, other arithmetic: 2.67 us -> none  [the longest x1 0.74 us: shards(): jnp.concatenate([attention_bias, norm_gain, norm_bias, reduce_bias[None]]...]
    squeeze x2 -> x0, local copies, waits for them, and re-layouts: 2 us -> none  [the longest x1 1.42 us: shards(): grad_narrow[12]]
where the time goes in v2:
time: 131 us
  Pallas kernels  130 us (99%)
    pallas_call x1, Pallas kernels, run_layer(): pl.pallas_call(kernel, out_shape=tuple((jax.ShapeDtypeStruct(shape, dtype...  126 us
    pallas_call x1, Pallas kernels, handed_out(): pl.pallas_call(copy_kernel, out_shape=tuple((jax.ShapeDtypeStruct(part.sh...  3.49 us

profile of v2, /device:TPU:0, one launch (start us, length us, event | category | flops | bytes accessed | tf_op | source)
XLA Modules:
  0.0 130.8 jit_solution(13203590070515166703)
XLA Ops:
  0.7 126.5 %shard_map.238 = (f32[6,16]{1,0:T(8,128)}, f32[3,16]{1,0:T(4,128)}, f32[3,16]{1,0:T(4,128)}, f32[1,16]{1,0:T(1,128)}, f32[1,64]{1,0:T(1,128)}, /*index=5*/bf16[2...) custom-call(s32[2]{0:T(128)} %refs_3_.1, ...), custom_call_target="tpu_custom_call" | custom-call | tf_op jit(solution)/shard_map/pallas_call | solution.py:786
  127.1 3.5 %shard_map.239 = (f32[6,16]{1,0:T(8,128)}, f32[3,16]{1,0:T(4,128)}, f32[3,16]{1,0:T(4,128)}, f32[1,16]{1,0:T(1,128)}, f32[1,64]{1,0:T(1,128)}, /*index=5*/bf16[2...) custom-call(f32[6,16]{1,0:T(8,128)} %get-tuple-element.36.refs_0_, ...), custom_call_target="tpu_custom_call" | custom-call | tf_op jit(solution)/shard_map/pallas_call | solution.py:814

commit v3 on v2

--- a/solution.py
+++ b/solution.py
@@ -19,12 +19,14 @@
 SQ, SK, SV, SO, CK, CV, CQ, CO, EXPAND, REDUCE = 0, 1, 2, 3, 4, 5, 6, 7, 8, 12
 BLOCKS = 16
 GATHER_CHUNKS = (
-    (0, 2, "xzyc"), (2, 4, "xzyc"), (4, 6, "zyxc"), (6, 8, "xzyc"),
-    (8, 10, "xzyc"), (10, 12, "xzyc"), (12, 14, "zyxc"), (14, 16, "xyzc"),
+    (0, 1, "zxyc"), (6, 8, "xyzc"), (2, 3, "zyxc"), (1, 2, "zxyc"), (8, 10, "xzyc"),
+    (12, 14, "xyzc"), (14, 15, "zxyc"), (3, 4, "zxyc"), (4, 6, "zxyc"), (10, 12, "zxyc"),
+    (15, 16, "zxyc"),
 )
 SCATTER_CHUNKS = (
-    (14, 16, "cyzx"), (12, 14, "cyzx"), (10, 12, "czyx"), (8, 10, "cyzx"),
-    (6, 8, "cyzx"), (4, 6, "cyzx"), (2, 4, "cxzy"), (0, 2, "cyxz"),
+    (15, 16, "cxyz"), (14, 15, "czyx"), (12, 14, "cyzx"), (10, 12, "cxyz"), (8, 10, "cyzx"),
+    (7, 8, "czxy"), (6, 7, "cyzx"), (4, 6, "cyxz"), (3, 4, "cyzx"), (0, 1, "cyxz"),
+    (1, 2, "cyxz"), (2, 3, "czyx"),
 )
 AXES = "zyxc"
 
@@ -278,9 +280,9 @@
     pl.semaphore_wait(barrier, len(peers))
 
     gathers = []
-    for number, (low, high, order) in enumerate(GATHER_CHUNKS):
+    for low, high, order in GATHER_CHUNKS:
         parts = [(s["w"], (slice(low, high),))]
-        if number == 0:
+        if low == 0:
             parts.append((s["small"], ()))
         gathers.append(Gather(links, place, grid, order, parts))
     memory_waits = [[] for _ in range(slots)]
@@ -352,10 +354,26 @@
         s["k"][...] = mm(x, weight(SK)).astype(BF16)
         s["v"][...] = (mm(x, weight(SV)) + bias(1)).astype(BF16)
 
-    def softmax(scores):
-        top = jnp.max(scores, axis=-1, keepdims=True)
-        weights = jnp.exp(scores - top)
-        return (weights * (1.0 / jnp.sum(weights, axis=-1, keepdims=True))).astype(BF16)
+    def attend(low_ref, share_ref, mixed_ref, queries, keys_in, values_in, keep, at, lanes):
+        scores = jnp.where(keep, mm_nt(stack(queries, scale), keys_in), NEG)
+        weights = jnp.exp(scores - jnp.max(scores, axis=-1, keepdims=True))
+        part = 1.0 / jnp.sum(weights, axis=-1, keepdims=True)
+        low = weights.astype(BF16)
+        low_ref[...] = low
+        share_ref[...] = part
+        mixed_ref[at, lanes] = unstack(mm(low, values_in) * part)
+
+    def attend_back(low_ref, share_ref, mixed, da, queries, keys_in, values_in):
+        low, part = low_ref[...], share_ref[...]
+        da = stack(da).astype(F32) * part
+        delta = jnp.sum(da * jnp.concatenate([mixed, mixed], axis=0), axis=-1, keepdims=True)
+        da = da.astype(BF16)
+        ds = (low.astype(F32) * (mm_nt(da, values_in) - delta)).astype(BF16)
+        return (
+            unstack(mm(ds, keys_in), scale).astype(BF16),
+            mm_tn(ds, stack(queries, scale)).astype(BF16),
+            mm_tn(low, da).astype(BF16),
+        )
 
     def self_attend():
         row = lax.broadcasted_iota(jnp.int32, (2 * span, span), 0) % span
@@ -365,10 +383,11 @@
             at = slice(slot * span, (slot + 1) * span)
             for pair in range(pairs):
                 lanes = slice(pair * LANES, (pair + 1) * LANES)
-                scores = mm_nt(stack(s["q"][at, lanes], scale), s["k"][at, lanes])
-                low = softmax(jnp.where(keep, scores, NEG))
-                s["ps"][slot, pair] = low
-                s["a"][at, lanes] = unstack(mm(low, s["v"][at, lanes])).astype(BF16)
+                attend(
+                    s["ps"].at[slot, pair], s["share"].at[slot, pair], s["af"],
+                    s["q"][at, lanes], s["k"][at, lanes], s["v"][at, lanes], keep, at, lanes,
+                )
+        s["a"][...] = s["af"][...].astype(BF16)
 
     def self_close():
         x = x_ref[...].reshape(rows, width).astype(F32)
@@ -382,14 +401,9 @@
         s["q2"][...] = (mm(s["h1b"][...], weight(CQ)) + bias(3)).astype(BF16)
 
     def cross_memory(slot):
-        for which, number in (("k2", CK), ("v2", CV)):
-            def body(part, carry, which=which, number=number):
-                value = mm(s["mem"][slot, part], weight(number))
-                if which == "v2":
-                    value = value + bias(4)
-                s[which][slot, part] = value.astype(BF16)
-                return carry
-            lax.fori_loop(0, members, body, 0)
+        items = s["mem"][slot].reshape(reach_span, width)
+        s["k2"][slot] = mm(items, weight(CK)).astype(BF16).reshape(members, chunk, width)
+        s["v2"][slot] = (mm(items, weight(CV)) + bias(4)).astype(BF16).reshape(members, chunk, width)
 
     def keys(name, slot, lanes):
         return s[name][slot, :, :, lanes].reshape(reach_span, LANES)
@@ -401,14 +415,15 @@
 
         def body(pair, carry):
             lanes = pl.ds(pl.multiple_of(pair * LANES, LANES), LANES)
-            scores = mm_nt(stack(s["q2"][at, lanes], scale), keys("k2", slot, lanes))
-            low = softmax(jnp.where(keep, scores, NEG))
-            s["pc"][slot, pair] = low
-            s["a2"][at, lanes] = unstack(mm(low, keys("v2", slot, lanes))).astype(BF16)
+            attend(
+                s["pc"].at[slot, pair], s["share2"].at[slot, pair], s["a2f"],
+                s["q2"][at, lanes], keys("k2", slot, lanes), keys("v2", slot, lanes), keep, at, lanes,
+            )
             return carry
         lax.fori_loop(0, pairs, body, 0)
 
     def cross_close():
+        s["a2"][...] = s["a2f"][...].astype(BF16)
         unit, rstd = normed(s["h1"][...] + mm(s["a2"][...], weight(CO)) + bias(5))
         s["n2"][...], s["d2"][...] = unit, rstd
         h2 = unit * bias(7) + bias(10)
@@ -464,31 +479,26 @@
         put_grad(CO, mm_tn(s["a2"][...], e2))
         s["da"][...] = mm_nt(e2, weight(CO)).astype(BF16)
 
-    def score_grad(low, grads):
-        weights = low.astype(F32)
-        return (weights * (grads - jnp.sum(weights * grads, axis=-1, keepdims=True))).astype(BF16)
-
     def cross_back(slot):
         at = slice(slot * span, (slot + 1) * span)
 
         def body(pair, carry):
             lanes = pl.ds(pl.multiple_of(pair * LANES, LANES), LANES)
-            da = stack(s["da"][at, lanes])
-            low = s["pc"][slot, pair]
-            ds = score_grad(low, mm_nt(da, keys("v2", slot, lanes)))
-            s["dq"][at, lanes] = unstack(mm(ds, keys("k2", slot, lanes)), scale).astype(BF16)
             shape = (members, chunk, LANES)
-            s["dk2"][slot, :, :, lanes] = mm_tn(ds, stack(s["q2"][at, lanes], scale)).astype(BF16).reshape(shape)
-            s["dv2"][slot, :, :, lanes] = mm_tn(low, da).astype(BF16).reshape(shape)
+            dq, dk, dv = attend_back(
+                s["pc"].at[slot, pair], s["share2"].at[slot, pair], s["a2f"][at, lanes], s["da"][at, lanes],
+                s["q2"][at, lanes], keys("k2", slot, lanes), keys("v2", slot, lanes),
+            )
+            s["dq"][at, lanes] = dq
+            s["dk2"][slot, :, :, lanes] = dk.reshape(shape)
+            s["dv2"][slot, :, :, lanes] = dv.reshape(shape)
             return carry
         lax.fori_loop(0, pairs, body, 0)
 
     def memory_grad(slot):
-        def body(part, carry):
-            value = mm_nt(s["dk2"][slot, part], weight(CK)) + mm_nt(s["dv2"][slot, part], weight(CV))
-            s["gmem"][slot, part] = value.astype(BF16)
-            return carry
-        lax.fori_loop(0, members, body, 0)
+        value = mm_nt(s["dk2"][slot].reshape(reach_span, width), weight(CK))
+        value += mm_nt(s["dv2"][slot].reshape(reach_span, width), weight(CV))
+        s["gmem"][slot] = value.astype(BF16).reshape(members, chunk, width)
 
     def send_memory_grad(slot):
         mine = gmem_ref.at[place.mem * slots + slot]
@@ -509,20 +519,11 @@
         put_grad(CQ, mm_tn(s["h1b"][...], dq))
 
     def memory_weight_grad():
-        for name, number in (("dk2", CK), ("dv2", CV)):
-            s["acc"][...] = jnp.zeros_like(s["acc"])
-
-            def body(part, carry, name=name):
-                for slot in range(slots):
-                    s["acc"][...] += mm_tn(s["mem"][slot, part], s[name][slot, part])
-                return carry
-            lax.fori_loop(0, members, body, 0)
-            put_grad(number, s["acc"][...])
-        total = jnp.zeros((1, width), F32)
-        for slot in range(slots):
-            for part in range(members):
-                total += column_sum(s["dv2"][slot, part])
-        s["rows_grad"][4:5, :] = total
+        items = s["mem"][...].reshape(slots * reach_span, width)
+        put_grad(CK, mm_tn(items, s["dk2"][...].reshape(slots * reach_span, width)))
+        dv = s["dv2"][...].reshape(slots * reach_span, width)
+        put_grad(CV, mm_tn(items, dv))
+        s["rows_grad"][4:5, :] = column_sum(dv)
 
     def self_open():
         dh1 = s["dr"][...] + mm_nt(s["dq"][...], weight(CQ))
@@ -538,12 +539,10 @@
             at = slice(slot * span, (slot + 1) * span)
             for pair in range(pairs):
                 lanes = slice(pair * LANES, (pair + 1) * LANES)
-                da = stack(s["da"][at, lanes])
-                low = s["ps"][slot, pair]
-                ds = score_grad(low, mm_nt(da, s["v"][at, lanes]))
-                s["dq"][at, lanes] = unstack(mm(ds, s["k"][at, lanes]), scale).astype(BF16)
-                s["dk"][at, lanes] = mm_tn(ds, stack(s["q"][at, lanes], scale)).astype(BF16)
-                s["dv"][at, lanes] = mm_tn(low, da).astype(BF16)
+                s["dq"][at, lanes], s["dk"][at, lanes], s["dv"][at, lanes] = attend_back(
+                    s["ps"].at[slot, pair], s["share"].at[slot, pair], s["af"][at, lanes], s["da"][at, lanes],
+                    s["q"][at, lanes], s["k"][at, lanes], s["v"][at, lanes],
+                )
 
     def self_grads():
         x = x_ref[...].reshape(rows, width)
@@ -623,91 +622,95 @@
             wait.wait_recv()
 
     s["rows_grad"][...] = jnp.zeros_like(s["rows_grad"])
-    gather(0, 1, 2, 3, 4, 5, 6, 7)
+    gather(0, 1, 2, 3, 4, 5, 6, 7, 8, 9, 10)
     send_memory(0, 0)
-    gather(0, 1, 3, 4, 2, 5, 7)
-    send_memory(0, 1)
-    gather(6, 2, 7, 0, 6, 1, 0, 2)
-    send_memory(1, 0)
-    gather(0)
+    gather(1, 4, 5, 0, 2, 1, 3, 5, 6, 7, 2, 0, 3, 8, 6, 7, 9, 0, 10, 2, 0)
     need(0)
     unpack_small()
-    gather(3, 2, 1, 6)
-    send_memory(1, 1)
-    gather(1)
-    need(1)
+    gather(3, 2, 8)
+    send_memory(0, 1)
+    gather(3)
+    need(2, 3)
     arrived(own_rows)
     self_project()
-    gather(4)
+    gather(6, 4)
     self_attend()
-    gather(3, 6)
+    gather(9, 6, 7, 10)
+    send_memory(1, 0)
+    gather(7)
+    need(7)
     self_close()
-    need(2)
+    gather(8)
+    send_memory(1, 1)
+    gather(8, 1, 4, 1)
+    need(1)
+    cross_query()
+    need(8)
     arrived([own_memory])
     arrived_memory(0)
     cross_memory(0)
-    gather(5, 3)
-    need(3)
-    cross_query()
     cross_attend(0)
     gather(4)
     arrived_memory(1)
     cross_memory(1)
+    gather(9)
     cross_attend(1)
-    gather(5, 4)
+    gather(5, 10, 9)
     cross_close()
     need(4)
     ff_up(0)
-    gather(7)
     ff_up(1)
+    need(9)
+    ff_up(2)
+    ff_up(3)
     gather(5)
     need(5)
-    ff_up(2)
-    ff_up(3)
+    ff_down(0)
+    gather(10)
+    ff_down(1)
     need(6)
-    ff_down(0)
-    ff_down(1)
-    gather(7)
-    need(7)
     ff_down(2)
+    need(10)
     ff_down(3)
     close()
     reduce_grad(3)
+    scatter(0)
     reduce_grad(2)
-    scatter(0)
+    scatter(1)
     reduce_grad(1)
     reduce_grad(0)
-    scatter(1)
+    scatter(2)
     ff_back(3)
     ff_back(2)
+    scatter(0, 1, 3)
+    ff_back(1)
     scatter(2)
-    ff_back(1)
     ff_back(0)
-    scatter(0, 3, 1)
+    scatter(4)
     cross_open()
-    scatter(2)
+    scatter(3, 5)
     cross_back(0)
-    scatter(3)
+    scatter(5, 0, 4)
     memory_grad(0)
     send_memory_grad(0)
-    scatter(0)
+    scatter(2, 1)
     cross_back(1)
-    scatter(1)
+    scatter(3, 0)
     memory_grad(1)
     send_memory_grad(1)
-    scatter(2)
     cross_query_grad()
-    scatter(4)
+    scatter(6)
     memory_weight_grad()
-    scatter(4, 5, 3, 0, 2)
+    scatter(7, 6, 4, 1, 5)
     self_open()
+    scatter(8, 3, 7)
     self_back()
-    scatter(5, 1)
+    scatter(8, 2, 0, 6)
     self_grads()
     pack_small()
-    scatter(6, 4, 7)
+    scatter(9, 10, 11)
     input_grad()
-    scatter(3, 6, 7, 0, 2, 1, 5, 3, 4, 6, 7, 4, 5, 7, 5, 6, 7, 6)
+    scatter(9, 10, 4, 11, 7, 3, 8, 6, 1, 5, 9, 2, 4, 10, 5, 7, 6, 11, 9, 10, 8, 11, 8, 7, 11, 9, 10)
     for work in scatters:
         while not work.over:
             work.step()
@@ -720,8 +723,8 @@
 
 def copy_count(grid, members, slots):
     count = 0
-    for index, (_, _, order) in enumerate(GATHER_CHUNKS):
-        count += sum(grid[axis] - 1 for axis in order) * (2 if index == 0 else 1)
+    for low, _, order in GATHER_CHUNKS:
+        count += sum(grid[axis] - 1 for axis in order) * (2 if low == 0 else 1)
     for index, (_, _, order) in enumerate(SCATTER_CHUNKS):
         count += sum(grid[axis] - 1 for axis in order) * (2 if index == len(SCATTER_CHUNKS) - 1 else 1)
     return count + (members - 1) * (2 * slots + slots)
@@ -751,6 +754,8 @@
         "land_small": landing_shapes(grid, SCATTER_CHUNKS[-1][2], (), (ROWS, LANES)),
         "pc": pltpu.VMEM((slots, pairs, 2 * span, members * chunk), BF16),
         "ps": pltpu.VMEM((slots, pairs, 2 * span, span), BF16),
+        "share": pltpu.VMEM((slots, pairs, 2 * span, 1), F32),
+        "share2": pltpu.VMEM((slots, pairs, 2 * span, 1), F32),
         "f": pltpu.VMEM((ff_blocks, rows, width), BF16),
         "slope": pltpu.VMEM((ff_blocks, rows, width), F32),
         "rows": pltpu.VMEM((ROWS, width), F32),
@@ -758,7 +763,6 @@
         "ebias": pltpu.VMEM((1, width * ff_blocks), F32),
         "ebias_grad": pltpu.VMEM((1, width * ff_blocks), F32),
         "tokens": pltpu.VMEM((8, LANES), F32),
-        "acc": pltpu.VMEM((width, width), F32),
         "d1": pltpu.VMEM((rows, 1), F32),
         "d2": pltpu.VMEM((rows, 1), F32),
         "send": pltpu.SemaphoreType.DMA((count,)),
@@ -769,7 +773,7 @@
         scratch[name] = pltpu.VMEM(mem_shape, BF16)
     for name in ("q", "k", "v", "a", "h1b", "q2", "a2", "h2b", "e", "da", "dq", "dk", "dv"):
         scratch[name] = pltpu.VMEM((rows, width), BF16)
-    for name in ("n1", "n2", "h1", "r3", "dr"):
+    for name in ("n1", "n2", "h1", "r3", "dr", "af", "a2f"):
         scratch[name] = pltpu.VMEM((rows, width), F32)
     for name in ("x", "dy", "y", "dx"):
         scratch[name] = pltpu.VMEM(x.shape, BF16)

time: 131 us -> 117 us (0.89)
  Pallas kernels: 130 us -> 116 us
    pallas_call x1, Pallas kernels: 126 us -> 113 us  [run_layer(): pl.pallas_call(kernel, out_shape=tuple((jax.ShapeDtypeStruct(shape, dtype...]
where the time goes in v3:
time: 117 us
  Pallas kernels  116 us (99%)
    pallas_call x1, Pallas kernels, run_layer(): pl.pallas_call(kernel, out_shape=tuple((jax.ShapeDtypeStruct(shape, dtype...  113 us
    pallas_call x1, Pallas kernels, handed_out(): pl.pallas_call(copy_kernel, out_shape=tuple((jax.ShapeDtypeStruct(part.sh...  3.49 us

profile of v3, /device:TPU:0, one launch (start us, length us, event | category | flops | bytes accessed | tf_op | source)
XLA Modules:
  0.0 117.1 jit_solution(4703122754704460211)
XLA Ops:
  0.7 112.8 %shard_map.238 = (f32[6,16]{1,0:T(8,128)}, f32[3,16]{1,0:T(4,128)}, f32[3,16]{1,0:T(4,128)}, f32[1,16]{1,0:T(1,128)}, f32[1,64]{1,0:T(1,128)}, /*index=5*/bf16[2...) custom-call(s32[2]{0:T(128)} %refs_3_.1, ...), custom_call_target="tpu_custom_call" | custom-call | tf_op jit(solution)/shard_map/pallas_call | solution.py:790
  113.5 3.5 %shard_map.239 = (f32[6,16]{1,0:T(8,128)}, f32[3,16]{1,0:T(4,128)}, f32[3,16]{1,0:T(4,128)}, f32[1,16]{1,0:T(1,128)}, f32[1,64]{1,0:T(1,128)}, /*index=5*/bf16[2...) custom-call(f32[6,16]{1,0:T(8,128)} %get-tuple-element.36.refs_0_, ...), custom_call_target="tpu_custom_call" | custom-call | tf_op jit(solution)/shard_map/pallas_call | solution.py:818

commit v4 on v3

--- a/solution.py
+++ b/solution.py
@@ -200,11 +200,10 @@
 
 def layer_kernel(
     sizes, grid,
-    lengths_ref, reaches_ref, routes_ref, all_lengths_ref, all_routes_ref,
-    attention_bias_ref, gain_ref, shift_ref, reduce_bias_ref, expand_bias_ref,
+    scalars_hbm, small_hbm,
     x_hbm, dy_hbm, in_hbm, out_hbm, expand_hbm, reduce_hbm, memory_ref,
-    grad_bias_ref, grad_gain_ref, grad_shift_ref, grad_reduce_bias_ref, grad_expand_bias_ref,
-    y_hbm, dx_hbm, grad_in_hbm, grad_out_hbm, grad_expand_hbm, grad_reduce_hbm, gmem_ref,
+    grad_small_refs,
+    y_ref, dx_ref, grad_in_ref, grad_out_ref, grad_expand_ref, grad_reduce_ref, gmem_ref,
     scratch,
 ):
     s = scratch
@@ -228,6 +227,8 @@
         return copy
 
     barrier = pltpu.get_barrier_semaphore()
+    lengths_ref, reaches_ref, routes_ref, all_lengths_ref, all_routes_ref = s["scalars"]
+    attention_bias_ref, gain_ref, shift_ref, reduce_bias_ref, expand_bias_ref = s["params"]
     peers = []
     for axis in "zy":
         peers += [place.device(axis, hop) for hop in range(1, sizes[axis])]
@@ -246,6 +247,8 @@
             parts += [(EXPAND + k, expand_ref.at[:, lanes]), (REDUCE + k, reduce_ref.at[:, lanes])]
         return sorted(parts, key=lambda part: part[0])
 
+    own_small = [local_copy(source, target) for source, target in zip(small_hbm, s["params"])]
+    own_small += [local_copy(source, target) for source, target in zip(scalars_hbm, s["scalars"])]
     own = [
         local_copy(part, s["w"].at[(number,) + here])
         for number, part in block_parts(in_hbm, out_hbm, expand_hbm, reduce_hbm)
@@ -258,6 +261,8 @@
         spot = spot * grid[axis] + at
     share = expand_bias_ref.shape[1]
     group, pieces = LANES // ROWS, LANES // share
+    for copy in own_small:
+        copy.wait()
     packet = s["packet"]
     packet[...] = jnp.zeros_like(packet)
     packet[0:6, 0:ROWS] = attention_bias_ref[...].astype(F32)
@@ -452,8 +457,7 @@
         unit, rstd = normed(s["r3"][...])
         y = unit * bias(8) + bias(11)
         y = jnp.where(live_rows(lambda slot: span), y, 0.0)
-        s["y"][...] = y.astype(BF16).reshape(x_ref.shape)
-        local_waits.append(local_copy(s["y"], y_hbm))
+        y_ref[...] = y.astype(BF16).reshape(x_ref.shape)
         dy = dy_ref[...].reshape(rows, width).astype(F32)
         dy = jnp.where(live_rows(lambda slot: lengths_ref[slot]), dy, 0.0)
         dr3 = norm_back(dy, unit, rstd, 2)
@@ -555,8 +559,7 @@
     def input_grad():
         total = s["dr"][...] + mm_nt(s["dq"][...], weight(SQ))
         total += mm_nt(s["dk"][...], weight(SK)) + mm_nt(s["dv"][...], weight(SV))
-        s["dx"][...] = total.astype(BF16).reshape(x_ref.shape)
-        local_waits.append(local_copy(s["dx"], dx_hbm))
+        dx_ref[...] = total.astype(BF16).reshape(x_ref.shape)
 
     def turned(value, lanes):
         return value if lanes == 0 else pltpu.roll(value, LANES - lanes, 1)
@@ -574,22 +577,20 @@
                 rest //= grid[axis]
             s["gsmall"][tuple(index)] = jnp.where(row == 13, extra, base).astype(BF16)
 
-    targets = dict(block_parts(grad_in_hbm, grad_out_hbm, grad_expand_hbm, grad_reduce_hbm))
+    targets = dict(block_parts(grad_in_ref, grad_out_ref, grad_expand_ref, grad_reduce_ref))
 
     def emit_weight(low, high):
         def emit(total):
-            s["stage"][low:high] = total / s["tokens"][0:1, 0:1]
             for number in range(low, high):
-                local_waits.append(local_copy(s["stage"].at[number], targets[number]))
+                targets[number][...] = total[number - low] / s["tokens"][0:1, 0:1]
         return emit
 
     def emit_small(total):
         value = total / s["tokens"][0:1, 0:1]
-        grad_bias_ref[...] = value[0:6, 0:ROWS]
-        grad_gain_ref[...] = value[6:9, 0:ROWS]
-        grad_shift_ref[...] = value[9:12, 0:ROWS]
-        grad_reduce_bias_ref[...] = value[12:13, 0:ROWS]
-        grad_expand_bias_ref[...] = value[13:14, 0:share]
+        first = 0
+        for target in grad_small_refs:
+            target[...] = value[first : first + target.shape[0], 0 : target.shape[1]]
+            first += target.shape[0]
 
     scatters = []
     for number, (low, high, order) in enumerate(SCATTER_CHUNKS):
@@ -747,7 +748,6 @@
         "packet": pltpu.VMEM((ROWS, LANES), F32),
         "gw": pltpu.VMEM((BLOCKS,) + place + (ROWS, width), BF16),
         "gsmall": pltpu.VMEM(place + (ROWS, LANES), BF16),
-        "stage": pltpu.VMEM((BLOCKS, ROWS, width), F32),
         "land": [
             landing_shapes(grid, order, (high - low,), (ROWS, width)) for low, high, order in SCATTER_CHUNKS
         ],
@@ -767,7 +767,9 @@
         "d2": pltpu.VMEM((rows, 1), F32),
         "send": pltpu.SemaphoreType.DMA((count,)),
         "recv": pltpu.SemaphoreType.DMA((count,)),
-        "local": pltpu.SemaphoreType.DMA((2 * BLOCKS + 5 + slots,)),
+        "local": pltpu.SemaphoreType.DMA((BLOCKS + 3 + slots + len(small) + len(scalars),)),
+        "scalars": [pltpu.SMEM(part.shape, part.dtype) for part in scalars],
+        "params": [pltpu.VMEM(part.shape, BF16) for part in small],
     }
     for name in ("mem", "k2", "v2", "dk2", "dv2", "gmem"):
         scratch[name] = pltpu.VMEM(mem_shape, BF16)
@@ -775,55 +777,56 @@
         scratch[name] = pltpu.VMEM((rows, width), BF16)
     for name in ("n1", "n2", "h1", "r3", "dr", "af", "a2f"):
         scratch[name] = pltpu.VMEM((rows, width), F32)
-    for name in ("x", "dy", "y", "dx"):
+    for name in ("x", "dy"):
         scratch[name] = pltpu.VMEM(x.shape, BF16)
     leaves, tree = jax.tree.flatten(scratch)
 
+    counts = (len(scalars), len(small), len(large), len(small), len(large))
+
     def kernel(*refs):
-        fixed = refs[: len(refs) - len(leaves)]
-        layer_kernel(sizes, grid, *fixed, jax.tree.unflatten(tree, refs[len(fixed) :]))
-
-    vmem, smem = pl.BlockSpec(memory_space=pltpu.VMEM), pl.BlockSpec(memory_space=pltpu.SMEM)
-    anywhere = pl.BlockSpec(memory_space=pl.ANY)
+        groups, at = [], 0
+        for size in counts:
+            groups.append(refs[at : at + size])
+            at += size
+        layer_kernel(
+            sizes, grid, groups[0], groups[1], *groups[2], groups[3], *groups[4],
+            jax.tree.unflatten(tree, refs[at:]),
+        )
+
+    anywhere, vmem = pl.BlockSpec(memory_space=pl.ANY), pl.BlockSpec(memory_space=pltpu.VMEM)
     outs = [(part.shape, F32) for part in small]
     outs += [(x.shape, BF16), (x.shape, BF16)] + [(part.shape, F32) for part in large[2:6]] + [(memory.shape, BF16)]
     return pl.pallas_call(
         kernel,
-        out_shape=tuple(jax.ShapeDtypeStruct(shape, dtype) for shape, dtype in outs),
-        in_specs=[smem] * len(scalars) + [vmem] * len(small) + [anywhere] * len(large),
-        out_specs=[vmem] * len(small) + [anywhere] * len(large),
+        out_shape=tuple(pltpu.VMEM(shape, dtype) for shape, dtype in outs),
+        in_specs=[anywhere] * sum(counts[:3]),
+        out_specs=[vmem] * sum(counts[3:]),
         scratch_shapes=leaves,
         compiler_params=pltpu.CompilerParams(
-            collective_id=0, has_side_effects=True, vmem_limit_bytes=62 << 20
+            collective_id=0, has_side_effects=True, vmem_limit_bytes=58 << 20
         ),
     )(*scalars, *small, *large)
 
 
 def copy_kernel(*refs):
-    count = (len(refs) - 1) // 3
-    sources, targets, held, sems = refs[:count], refs[count : 2 * count], refs[2 * count : -1], refs[-1]
-    inward = [pltpu.make_async_copy(sources[n], held[n], sems.at[0, n]) for n in range(count)]
-    outward = [pltpu.make_async_copy(held[n], targets[n], sems.at[1, n]) for n in range(count)]
-    for copy in inward:
+    count, sems = len(refs) // 2, refs[-1]
+    copies = [pltpu.make_async_copy(refs[n], refs[count + n], sems.at[n]) for n in range(count)]
+    for copy in copies:
         copy.start()
-    for came, goes in zip(inward, outward):
-        came.wait()
-        goes.start()
-    for copy in outward:
+    for copy in copies:
         copy.wait()
 
 
 def handed_out(results):
-    anywhere = pl.BlockSpec(memory_space=pl.ANY)
+    anywhere, vmem = pl.BlockSpec(memory_space=pl.ANY), pl.BlockSpec(memory_space=pltpu.VMEM)
     return pl.pallas_call(
         copy_kernel,
-        out_shape=tuple(jax.ShapeDtypeStruct(part.shape, part.dtype) for part in results),
-        in_specs=[anywhere] * len(results),
+        out_shape=tuple(pltpu.HBM(part.shape, part.dtype) for part in results),
+        in_specs=[vmem] * len(results),
         out_specs=[anywhere] * len(results),
-        scratch_shapes=[pltpu.VMEM(part.shape, part.dtype) for part in results]
-        + [pltpu.SemaphoreType.DMA((2, len(results)))],
-        compiler_params=pltpu.CompilerParams(vmem_limit_bytes=62 << 20),
-    )(*results)
+        scratch_shapes=[pltpu.SemaphoreType.DMA((len(results),))],
+        compiler_params=pltpu.CompilerParams(vmem_limit_bytes=32 << 20),
+    )(*(pltpu.with_memory_space_constraint(part, pltpu.VMEM) for part in results))
 
 
 def shards(

time: 117 us -> 113 us (0.966)
  Pallas kernels: 116 us -> 112 us
    pallas_call x2, Pallas kernels: 116 us -> 112 us  [the longest x1 111 us: run_layer(): pl.pallas_call(kernel, out_shape=tuple((pltpu.VMEM(shape, dtype) for shap...]
where the time goes in v4:
time: 113 us
  Pallas kernels  112 us (99%)
    pallas_call x1, Pallas kernels, run_layer(): pl.pallas_call(kernel, out_shape=tuple((pltpu.VMEM(shape, dtype) for shap...  111 us

profile of v4, /device:TPU:0, one launch (start us, length us, event | category | flops | bytes accessed | tf_op | source)
XLA Modules:
  0.0 113.2 jit_solution(10661101622443854794)
XLA Ops:
  0.7 110.6 %shard_map.238 = (f32[6,16]{1,0:T(8,128)S(1)}, f32[3,16]{1,0:T(4,128)S(1)}, f32[3,16]{1,0:T(4,128)S(1)}, f32[1,16]{1,0:T(1,128)S(1)}, f32[1,64]{1,0:T(1,128)S(1)...) custom-call(s32[2]{0:T(128)} %refs_3_.1, ...), custom_call_target="tpu_custom_call" | custom-call | tf_op jit(solution)/shard_map/pallas_call | solution.py:799
  111.3 1.8 %shard_map.239 = (f32[6,16]{1,0:T(8,128)}, f32[3,16]{1,0:T(4,128)}, f32[3,16]{1,0:T(4,128)}, f32[1,16]{1,0:T(1,128)}, f32[1,64]{1,0:T(1,128)}, /*index=5*/bf16[2...) custom-call(f32[6,16]{1,0:T(8,128)S(1)} %get-tuple-element.36.refs_0, ...), custom_call_target="tpu_custom_call" | custom-call | tf_op jit(solution)/shard_map/pallas_call | solution.py:822

commit v5 on v4

--- a/solution.py
+++ b/solution.py
@@ -19,14 +19,14 @@
 SQ, SK, SV, SO, CK, CV, CQ, CO, EXPAND, REDUCE = 0, 1, 2, 3, 4, 5, 6, 7, 8, 12
 BLOCKS = 16
 GATHER_CHUNKS = (
-    (0, 1, "zxyc"), (6, 8, "xyzc"), (2, 3, "zyxc"), (1, 2, "zxyc"), (8, 10, "xzyc"),
-    (12, 14, "xyzc"), (14, 15, "zxyc"), (3, 4, "zxyc"), (4, 6, "zxyc"), (10, 12, "zxyc"),
-    (15, 16, "zxyc"),
+    (2, 3, "xzyc"), (0, 1, "zxyc"), (1, 2, "zxyc"), (6, 8, "zyxc"), (3, 4, "zxyc"),
+    (4, 6, "xzyc"), (10, 12, "xzyc"), (12, 13, "xzyc"), (15, 16, "yxzc"), (8, 10, "zyxc"),
+    (14, 15, "zxyc"), (13, 14, "xyzc"),
 )
 SCATTER_CHUNKS = (
-    (15, 16, "cxyz"), (14, 15, "czyx"), (12, 14, "cyzx"), (10, 12, "cxyz"), (8, 10, "cyzx"),
-    (7, 8, "czxy"), (6, 7, "cyzx"), (4, 6, "cyxz"), (3, 4, "cyzx"), (0, 1, "cyxz"),
-    (1, 2, "cyxz"), (2, 3, "czyx"),
+    (15, 16, "cyzx"), (14, 15, "czyx"), (13, 14, "cyzx"), (12, 13, "cxzy"), (10, 12, "cxyz"),
+    (8, 10, "cyzx"), (7, 8, "cyzx"), (6, 7, "cyzx"), (5, 6, "cyxz"), (4, 5, "cyxz"),
+    (3, 4, "cyxz"), (0, 1, "cyxz"), (1, 2, "czyx"), (2, 3, "cyzx"),
 )
 AXES = "zyxc"
 
@@ -425,7 +425,7 @@
                 s["q2"][at, lanes], keys("k2", slot, lanes), keys("v2", slot, lanes), keep, at, lanes,
             )
             return carry
-        lax.fori_loop(0, pairs, body, 0)
+        lax.fori_loop(0, pairs, body, 0, unroll=4)
 
     def cross_close():
         s["a2"][...] = s["a2f"][...].astype(BF16)
@@ -497,7 +497,7 @@
             s["dk2"][slot, :, :, lanes] = dk.reshape(shape)
             s["dv2"][slot, :, :, lanes] = dv.reshape(shape)
             return carry
-        lax.fori_loop(0, pairs, body, 0)
+        lax.fori_loop(0, pairs, body, 0, unroll=4)
 
     def memory_grad(slot):
         value = mm_nt(s["dk2"][slot].reshape(reach_span, width), weight(CK))
@@ -623,95 +623,94 @@
             wait.wait_recv()
 
     s["rows_grad"][...] = jnp.zeros_like(s["rows_grad"])
-    gather(0, 1, 2, 3, 4, 5, 6, 7, 8, 9, 10)
+    gather(1, 0, 2, 11, 6, 3)
     send_memory(0, 0)
-    gather(1, 4, 5, 0, 2, 1, 3, 5, 6, 7, 2, 0, 3, 8, 6, 7, 9, 0, 10, 2, 0)
-    need(0)
+    gather(11, 1, 2, 4, 7, 0, 5, 8, 3)
+    send_memory(0, 1)
+    gather(1, 10, 5, 2, 4, 0, 10, 9, 8, 3, 7, 1, 6, 4)
+    send_memory(1, 0)
+    send_memory(1, 1)
+    gather(5, 1)
+    need(1)
     unpack_small()
-    gather(3, 2, 8)
-    send_memory(0, 1)
-    gather(3)
-    need(2, 3)
+    gather(2, 0, 0, 2, 8, 4, 9, 3, 10, 4)
+    need(0, 2)
     arrived(own_rows)
     self_project()
-    gather(6, 4)
+    gather(5, 3)
     self_attend()
-    gather(9, 6, 7, 10)
-    send_memory(1, 0)
+    gather(11)
+    need(4)
+    self_close()
     gather(7)
-    need(7)
-    self_close()
-    gather(8)
-    send_memory(1, 1)
-    gather(8, 1, 4, 1)
-    need(1)
+    need(3)
     cross_query()
-    need(8)
+    gather(9, 5)
+    need(5)
     arrived([own_memory])
     arrived_memory(0)
     cross_memory(0)
+    gather(6)
     cross_attend(0)
-    gather(4)
+    gather(10)
     arrived_memory(1)
     cross_memory(1)
-    gather(9)
+    gather(7, 8)
     cross_attend(1)
-    gather(5, 10, 9)
+    gather(9, 10, 6, 7)
     cross_close()
-    need(4)
+    gather(11, 8, 9)
+    need(9)
     ff_up(0)
     ff_up(1)
-    need(9)
+    gather(6)
+    need(6)
     ff_up(2)
     ff_up(3)
-    gather(5)
-    need(5)
+    need(7)
     ff_down(0)
-    gather(10)
+    gather(11)
+    need(11)
     ff_down(1)
-    need(6)
+    need(10)
     ff_down(2)
-    need(10)
+    need(8)
     ff_down(3)
     close()
     reduce_grad(3)
-    scatter(0)
     reduce_grad(2)
-    scatter(1)
     reduce_grad(1)
     reduce_grad(0)
-    scatter(2)
+    scatter(3, 1, 2)
     ff_back(3)
     ff_back(2)
-    scatter(0, 1, 3)
+    scatter(4, 0, 3, 1)
     ff_back(1)
     scatter(2)
     ff_back(0)
-    scatter(4)
     cross_open()
-    scatter(3, 5)
+    scatter(5, 6, 0, 4)
     cross_back(0)
-    scatter(5, 0, 4)
+    scatter(6, 2)
     memory_grad(0)
     send_memory_grad(0)
-    scatter(2, 1)
+    scatter(5, 3)
     cross_back(1)
-    scatter(3, 0)
+    scatter(0, 4)
     memory_grad(1)
     send_memory_grad(1)
     cross_query_grad()
-    scatter(6)
+    scatter(7, 6, 1)
     memory_weight_grad()
-    scatter(7, 6, 4, 1, 5)
+    scatter(8, 7, 5)
     self_open()
-    scatter(8, 3, 7)
+    scatter(10, 8)
     self_back()
-    scatter(8, 2, 0, 6)
     self_grads()
     pack_small()
-    scatter(9, 10, 11)
+    scatter(12, 10, 7, 13, 9, 1, 2, 12, 6, 13, 11, 11, 9, 10, 0, 4, 8, 3, 11, 13, 1, 10, 8, 12, 6, 9)
     input_grad()
-    scatter(9, 10, 4, 11, 7, 3, 8, 6, 1, 5, 9, 2, 4, 10, 5, 7, 6, 11, 9, 10, 8, 11, 8, 7, 11, 9, 10)
+    scatter(11, 5, 12, 4, 9, 13, 0, 7, 10, 3, 8, 5, 7, 11, 2, 12, 13, 9)
     for work in scatters:
         while not work.over:
             work.step()

time: 113 us -> 108 us (0.956)
  Pallas kernels: 112 us -> 107 us
    pallas_call x1, Pallas kernels: 111 us -> 105 us  [run_layer(): pl.pallas_call(kernel, out_shape=tuple((pltpu.VMEM(shape, dtype) for shap...]
where the time goes in v5:
time: 108 us
  Pallas kernels  107 us (99%)
    pallas_call x1, Pallas kernels, run_layer(): pl.pallas_call(kernel, out_shape=tuple((pltpu.VMEM(shape, dtype) for shap...  105 us

profile of v5, /device:TPU:0, one launch (start us, length us, event | category | flops | bytes accessed | tf_op | source)
XLA Modules:
  0.0 108.0 jit_solution(4534524229702710482)
XLA Ops:
  0.7 105.4 %shard_map.238 = (f32[6,16]{1,0:T(8,128)S(1)}, f32[3,16]{1,0:T(4,128)S(1)}, f32[3,16]{1,0:T(4,128)S(1)}, f32[1,16]{1,0:T(1,128)S(1)}, f32[1,64]{1,0:T(1,128)S(1)...) custom-call(s32[2]{0:T(128)} %refs_3_.1, ...), custom_call_target="tpu_custom_call" | custom-call | tf_op jit(solution)/shard_map/pallas_call | solution.py:798
  106.0 1.8 %shard_map.239 = (f32[6,16]{1,0:T(8,128)}, f32[3,16]{1,0:T(4,128)}, f32[3,16]{1,0:T(4,128)}, f32[1,16]{1,0:T(1,128)}, f32[1,64]{1,0:T(1,128)}, /*index=5*/bf16[2...) custom-call(f32[6,16]{1,0:T(8,128)S(1)} %get-tuple-element.36.refs_0, ...), custom_call_target="tpu_custom_call" | custom-call | tf_op jit(solution)/shard_map/pallas_call | solution.py:821

commit v6 on v5

--- a/solution.py
+++ b/solution.py
@@ -19,14 +19,14 @@
 SQ, SK, SV, SO, CK, CV, CQ, CO, EXPAND, REDUCE = 0, 1, 2, 3, 4, 5, 6, 7, 8, 12
 BLOCKS = 16
 GATHER_CHUNKS = (
-    (2, 3, "xzyc"), (0, 1, "zxyc"), (1, 2, "zxyc"), (6, 8, "zyxc"), (3, 4, "zxyc"),
-    (4, 6, "xzyc"), (10, 12, "xzyc"), (12, 13, "xzyc"), (15, 16, "yxzc"), (8, 10, "zyxc"),
-    (14, 15, "zxyc"), (13, 14, "xyzc"),
+    (1, 2, "zxyc"), (3, 4, "xyzc"), (0, 1, "xzyc"), (2, 3, "zxyc"), (12, 14, "zyxc"),
+    (4, 6, "xyzc"), (15, 16, "xzyc"), (6, 8, "zxyc"), (10, 12, "zxyc"), (14, 15, "xyzc"),
+    (8, 10, "xyzc"),
 )
 SCATTER_CHUNKS = (
-    (15, 16, "cyzx"), (14, 15, "czyx"), (13, 14, "cyzx"), (12, 13, "cxzy"), (10, 12, "cxyz"),
-    (8, 10, "cyzx"), (7, 8, "cyzx"), (6, 7, "cyzx"), (5, 6, "cyxz"), (4, 5, "cyxz"),
-    (3, 4, "cyxz"), (0, 1, "cyxz"), (1, 2, "czyx"), (2, 3, "cyzx"),
+    (15, 16, "czyx"), (14, 15, "czyx"), (12, 14, "cxyz"), (10, 12, "czyx"), (8, 10, "cyzx"),
+    (7, 8, "cyxz"), (6, 7, "cyzx"), (4, 6, "cyxz"), (3, 4, "czxy"), (0, 1, "cyxz"),
+    (1, 2, "czyx"), (2, 3, "cyxz"),
 )
 AXES = "zyxc"
 
@@ -41,6 +41,31 @@
 
 def mm_tn(left, right):
     return lax.dot_general(left, right, (((0,), (0,)), ((), ())), preferred_element_type=F32)
+
+
+def only_if(condition, action):
+    if condition is None:
+        action()
+    else:
+        pl.when(condition)(action)
+
+
+class Landing:
+    def __init__(self, copy, lands):
+        self.copy, self.lands = copy, lands
+
+    def wait_recv(self):
+        only_if(self.lands, self.copy.wait_recv)
+
+
+def steps_of(grid, order):
+    steps = []
+    for axis in order:
+        if axis == "z" and grid["z"] == 4:
+            steps += ["z", "Z"]
+        elif grid[axis] > 1:
+            steps.append(axis)
+    return steps
 
 
 class Links:
@@ -51,22 +76,25 @@
         self.used += 1
         return self.send_sems.at[self.used - 1], self.recv_sems.at[self.used - 1]
 
-    def copy(self, source, target, landing, device):
+    def copy(self, source, target, landing, device, sends=None, lands=None):
         send, recv = self.pair()
         out = pltpu.make_async_remote_copy(
             src_ref=source, dst_ref=target, send_sem=send, recv_sem=recv,
             device_id=device, device_id_type=MESH,
         )
-        out.start()
-        self.sent.append(out)
-        return pltpu.make_async_remote_copy(
-            src_ref=source, dst_ref=landing, send_sem=send, recv_sem=recv,
-            device_id=device, device_id_type=MESH,
+        only_if(sends, out.start)
+        self.sent.append((sends, out))
+        return Landing(
+            pltpu.make_async_remote_copy(
+                src_ref=source, dst_ref=landing, send_sem=send, recv_sem=recv,
+                device_id=device, device_id_type=MESH,
+            ),
+            lands,
         )
 
     def finish(self):
-        for out in self.sent:
-            out.wait_send()
+        for sends, out in self.sent:
+            only_if(sends, out.wait_send)
 
 
 class Place:
@@ -79,6 +107,15 @@
             "x": mem // sizes["c"], "c": mem % sizes["c"],
         }
 
+    def on_line(self):
+        z = self.at["z"]
+        side = z // 2
+        middle = (z == 1) | (z == 2)
+        return middle, jnp.logical_not(middle), z + 1 - 2 * (z % 2), 2 - side, 3 * (1 - side), 2 * (1 - side)
+
+    def at_z(self, z):
+        return (z * self.sizes["y"] + self.at["y"], self.mem)
+
     def shifted(self, axis, step):
         size = self.sizes[axis]
         return lax.rem(self.at[axis] + (step % size), size)
@@ -94,9 +131,38 @@
 
 
 class Gather:
+    def index(self, known):
+        return {
+            axis: slice(None) if axis in known else (self.place.at[axis] if self.grid[axis] > 1 else 0)
+            for axis in AXES
+        }
+
+    def line_step(self, axis, known):
+        middle, end, pair, far_middle, far_end, far_first = self.place.on_line()
+
+        def send(source_z, landing_z, target_z, sends, lands):
+            source, landing = self.index(known), self.index(known)
+            source["z"], landing["z"] = source_z, landing_z
+            for ref, lead in self.parts:
+                here = block_view(ref, lead, source)
+                self.waits.append(
+                    self.links.copy(
+                        here, here, block_view(ref, lead, landing), self.place.at_z(target_z), sends, lands
+                    )
+                )
+
+        z = self.place.at["z"]
+        if axis == "z":
+            send(z, far_end, far_middle, end, middle)
+            send(z, far_middle, far_middle, middle, middle)
+            send(z, pair, pair, None, None)
+        else:
+            both = pl.ds(far_first, 2)
+            send(both, both, pair, middle, end)
+
     def __init__(self, links, place, grid, order, parts):
         self.links, self.place, self.parts = links, place, parts
-        self.order = [axis for axis in order if grid[axis] > 1]
+        self.order = steps_of(grid, order)
         self.grid, self.waits, self.done = grid, [], 0
 
     @property
@@ -112,14 +178,12 @@
         if self.done < len(self.order):
             axis = self.order[self.done]
             known = self.order[: self.done]
+            if axis in "zZ" and "Z" in self.order:
+                self.line_step(axis, known)
+                self.done += 1
+                return
             for hop in range(1, self.grid[axis]):
-                mine, theirs = {}, {}
-                for other in AXES:
-                    if other in known:
-                        mine[other] = theirs[other] = slice(None)
-                    else:
-                        at = self.place.at[other] if self.grid[other] > 1 else 0
-                        mine[other] = theirs[other] = at
+                mine, theirs = self.index(known), self.index(known)
                 theirs[axis] = self.place.shifted(axis, -hop)
                 for ref, lead in self.parts:
                     self.waits.append(
@@ -134,7 +198,7 @@
 class Scatter:
     def __init__(self, links, place, grid, order, parts, landings, emit):
         self.links, self.place, self.parts, self.landings = links, place, parts, landings
-        self.order = [axis for axis in order if grid[axis] > 1]
+        self.order = steps_of(grid, order)
         self.grid, self.waits, self.done, self.emit = grid, [], 0, emit
 
     def index(self, known):
@@ -154,19 +218,21 @@
         for wait in self.waits:
             wait.wait_recv()
         self.waits = []
-        if self.done > 0:
+        if self.done > 0 and self.order[self.done - 1] == "z" and "Z" in self.order:
+            self.line_add()
+        elif self.done > 0:
             axis = self.order[self.done - 1]
             last = self.done == len(self.order)
             index = self.index(self.order[: self.done])
             for number, (ref, lead) in enumerate(self.parts):
                 where = tuple(lead) + tuple(index[name] for name in AXES)
                 landed = self.landings[number][self.done - 1]
-                if self.grid[axis] == 2 and not last:
+                if landed.shape[0] == 1 and not last:
                     ref[where] = ref[where] + landed[0]
                     continue
                 total = ref[where].astype(F32)
-                for hop in range(1, self.grid[axis]):
-                    total += landed[hop - 1].astype(F32)
+                for hop in range(landed.shape[0]):
+                    total += landed[hop].astype(F32)
                 if last:
                     self.emit[number](total)
                 else:
@@ -174,6 +240,10 @@
         if self.done < len(self.order):
             axis = self.order[self.done]
             known = self.order[: self.done]
+            if axis in "zZ" and "Z" in self.order:
+                self.line_step(axis, known)
+                self.done += 1
+                return
             for hop in range(1, self.grid[axis]):
                 theirs = self.index(known)
                 theirs[axis] = self.place.shifted(axis, hop)
@@ -187,14 +257,57 @@
         self.done += 1
 
 
+    def line_step(self, axis, known):
+        middle, end, pair, far_middle, far_end, far_first = self.place.on_line()
+        known = [name for name in known if name != "z"]
+
+        def send(source_z, landing, target_z, sends, lands):
+            source = self.index(known)
+            source["z"] = source_z
+            for number, (ref, lead) in enumerate(self.parts):
+                held = landing(self.landings[number])
+                self.waits.append(
+                    self.links.copy(
+                        block_view(ref, lead, source), held, held, self.place.at_z(target_z), sends, lands
+                    )
+                )
+
+        first = self.order.index("z")
+        if axis == "z":
+            send(pl.ds(far_first, 2), lambda held: held[first], pair, end, middle)
+            self.pair_waits = []
+            waits, self.waits = self.waits, []
+            send(pair, lambda held: held[first + 1].at[0], pair, None, None)
+            self.pair_waits, self.waits = self.waits, waits
+        else:
+            send(far_middle, lambda held: held[first + 1].at[1], far_middle, middle, middle)
+            send(far_end, lambda held: held[first + 1].at[1], far_end, middle, end)
+            self.waits += self.pair_waits
+
+    def line_add(self):
+        middle, _, _, _, _, far_first = self.place.on_line()
+        first = self.order.index("z")
+        index = self.index(self.order[:first])
+        index["z"] = pl.ds(far_first, 2)
+
+        @pl.when(middle)
+        def _():
+            for number, (ref, lead) in enumerate(self.parts):
+                where = tuple(lead) + tuple(index[name] for name in AXES)
+                ref[where] = ref[where] + self.landings[number][first][...]
+
+
 def landing_shapes(grid, order, lead_shape, tail_shape):
     shapes, left = [], {axis: grid[axis] for axis in AXES}
-    for axis in order:
-        if grid[axis] == 1:
-            continue
-        left[axis] = 1
+    steps = steps_of(grid, order)
+    for axis in steps:
+        left[axis.lower()] = 1
         kept = tuple(left[name] for name in AXES if left[name] > 1)
-        shapes.append(pltpu.VMEM((grid[axis] - 1,) + lead_shape + kept + tail_shape, BF16))
+        if axis == "z" and "Z" in steps:
+            shape = lead_shape + (2,) + kept + tail_shape
+        else:
+            shape = (2 if axis == "Z" else grid[axis] - 1,) + lead_shape + kept + tail_shape
+        shapes.append(pltpu.VMEM(shape, BF16))
     return shapes
 
 
@@ -623,94 +736,93 @@
             wait.wait_recv()
 
     s["rows_grad"][...] = jnp.zeros_like(s["rows_grad"])
-    gather(1, 0, 2, 11, 6, 3)
+    gather(2, 3, 5, 0, 4, 1, 6, 8, 10, 9, 7)
     send_memory(0, 0)
-    gather(11, 1, 2, 4, 7, 0, 5, 8, 3)
+    gather(2, 3, 0, 4, 1, 5, 10, 8, 6, 7, 3, 9, 1, 0, 4, 2, 8, 5, 3, 6, 10, 7, 0, 1)
     send_memory(0, 1)
-    gather(1, 10, 5, 2, 4, 0, 10, 9, 8, 3, 7, 1, 6, 4)
+    gather(2, 7, 6, 5)
     send_memory(1, 0)
+    gather(0, 2)
     send_memory(1, 1)
-    gather(5, 1)
-    need(1)
+    gather(4, 3, 0, 2, 1, 9, 10, 3, 1, 8)
+    need(2)
     unpack_small()
-    gather(2, 0, 0, 2, 8, 4, 9, 3, 10, 4)
-    need(0, 2)
+    gather(7)
+    need(0, 3)
     arrived(own_rows)
     self_project()
-    gather(5, 3)
+    gather(5)
     self_attend()
-    gather(11)
-    need(4)
+    need(1)
     self_close()
     gather(7)
-    need(3)
+    need(7)
     cross_query()
-    gather(9, 5)
+    gather(6, 5, 9)
     need(5)
     arrived([own_memory])
     arrived_memory(0)
     cross_memory(0)
-    gather(6)
     cross_attend(0)
-    gather(10)
     arrived_memory(1)
     cross_memory(1)
-    gather(7, 8)
+    gather(10, 8)
     cross_attend(1)
-    gather(9, 10, 6, 7)
+    gather(9, 6, 4)
     cross_close()
-    gather(11, 8, 9)
+    gather(10)
+    need(10)
+    ff_up(0)
+    gather(8)
+    ff_up(1)
+    need(8)
+    ff_up(2)
+    gather(9)
+    ff_up(3)
+    gather(4)
+    need(4)
+    ff_down(0)
+    ff_down(1)
     need(9)
-    ff_up(0)
-    ff_up(1)
-    gather(6)
+    ff_down(2)
     need(6)
-    ff_up(2)
-    ff_up(3)
-    need(7)
-    ff_down(0)
-    gather(11)
-    need(11)
-    ff_down(1)
-    need(10)
-    ff_down(2)
-    need(8)
     ff_down(3)
     close()
     reduce_grad(3)
+    scatter(0)
     reduce_grad(2)
     reduce_grad(1)
     reduce_grad(0)
-    scatter(3, 1, 2)
+    scatter(2)
     ff_back(3)
     ff_back(2)
-    scatter(4, 0, 3, 1)
     ff_back(1)
-    scatter(2)
     ff_back(0)
+    scatter(3, 0, 4, 2)
     cross_open()
-    scatter(5, 6, 0, 4)
+    scatter(1)
     cross_back(0)
-    scatter(6, 2)
+    scatter(3)
     memory_grad(0)
     send_memory_grad(0)
-    scatter(5, 3)
+    scatter(4)
     cross_back(1)
-    scatter(0, 4)
     memory_grad(1)
     send_memory_grad(1)
+    scatter(5, 1)
     cross_query_grad()
-    scatter(7, 6, 1)
+    scatter(2, 6)
     memory_weight_grad()
-    scatter(8, 7, 5)
+    scatter(5, 7)
     self_open()
-    scatter(10, 8)
+    scatter(3, 4, 6, 8, 7)
     self_back()
+    scatter(8, 0, 1)
     self_grads()
     pack_small()
-    scatter(12, 10, 7, 13, 9, 1, 2, 12, 6, 13, 11, 11, 9, 10, 0, 4, 8, 3, 11, 13, 1, 10, 8, 12, 6, 9)
+    scatter(11, 9, 6, 5, 10, 11, 10, 4, 9, 0, 2, 8, 7, 1, 11, 5, 10, 3, 6, 9, 7, 0, 8, 11, 2, 1, 4)
     input_grad()
-    scatter(11, 5, 12, 4, 9, 13, 0, 7, 10, 3, 8, 5, 7, 11, 2, 12, 13, 9)
+    scatter(9, 5, 10, 7, 8, 3, 6, 11, 9, 10, 0, 5, 2, 6, 4, 7, 8, 3, 11, 1, 10, 9)
     for work in scatters:
         while not work.over:
             work.step()
@@ -722,11 +834,12 @@
 
 
 def copy_count(grid, members, slots):
-    count = 0
-    for low, _, order in GATHER_CHUNKS:
-        count += sum(grid[axis] - 1 for axis in order) * (2 if low == 0 else 1)
-    for index, (_, _, order) in enumerate(SCATTER_CHUNKS):
-        count += sum(grid[axis] - 1 for axis in order) * (2 if index == len(SCATTER_CHUNKS) - 1 else 1)
+    def copies(order):
+        steps = steps_of(grid, order)
+        return sum(2 if axis in "zZ" and "Z" in steps else grid[axis] - 1 for axis in steps)
+
+    count = sum(copies(order) * (2 if low == 0 else 1) for low, _, order in GATHER_CHUNKS)
+    count += sum(copies(order) for _, _, order in SCATTER_CHUNKS) + copies(SCATTER_CHUNKS[-1][2])
     return count + (members - 1) * (2 * slots + slots)
 
 

time: 108 us -> 104 us (0.963)
  Pallas kernels: 107 us -> 103 us
    pallas_call x1, Pallas kernels: 105 us -> 101 us  [run_layer(): pl.pallas_call(kernel, out_shape=tuple((pltpu.VMEM(shape, dtype) for shap...]
where the time goes in v6:
time: 104 us
  Pallas kernels  103 us (99%)
    pallas_call x1, Pallas kernels, run_layer(): pl.pallas_call(kernel, out_shape=tuple((pltpu.VMEM(shape, dtype) for shap...  101 us

profile of v6, /device:TPU:0, one launch (start us, length us, event | category | flops | bytes accessed | tf_op | source)
XLA Modules:
  0.0 103.8 jit_solution(9451338175025890161)
XLA Ops:
  0.7 101.2 %shard_map.238 = (f32[6,16]{1,0:T(8,128)S(1)}, f32[3,16]{1,0:T(4,128)S(1)}, f32[3,16]{1,0:T(4,128)S(1)}, f32[1,16]{1,0:T(1,128)S(1)}, f32[1,64]{1,0:T(1,128)S(1)...) custom-call(s32[2]{0:T(128)} %refs_3_.1, ...), custom_call_target="tpu_custom_call" | custom-call | tf_op jit(solution)/shard_map/pallas_call | solution.py:911
  101.9 1.8 %shard_map.239 = (f32[6,16]{1,0:T(8,128)}, f32[3,16]{1,0:T(4,128)}, f32[3,16]{1,0:T(4,128)}, f32[1,16]{1,0:T(1,128)}, f32[1,64]{1,0:T(1,128)}, /*index=5*/bf16[2...) custom-call(f32[6,16]{1,0:T(8,128)S(1)} %get-tuple-element.36.refs_0, ...), custom_call_target="tpu_custom_call" | custom-call | tf_op jit(solution)/shard_map/pallas_call | solution.py:934

commit v7 on v6

--- a/solution.py
+++ b/solution.py
@@ -24,9 +24,9 @@
     (8, 10, "xyzc"),
 )
 SCATTER_CHUNKS = (
-    (15, 16, "czyx"), (14, 15, "czyx"), (12, 14, "cxyz"), (10, 12, "czyx"), (8, 10, "cyzx"),
-    (7, 8, "cyxz"), (6, 7, "cyzx"), (4, 6, "cyxz"), (3, 4, "czxy"), (0, 1, "cyxz"),
-    (1, 2, "czyx"), (2, 3, "cyxz"),
+    (15, 16, "cxyz"), (14, 15, "czyx"), (12, 14, "cyzx"), (10, 12, "czyx"), (8, 10, "cyzx"),
+    (7, 8, "cyzx"), (6, 7, "cyzx"), (4, 6, "cyxz"), (3, 4, "cyxz"), (0, 1, "cyxz"),
+    (1, 2, "cxzy"), (2, 3, "czyx"),
 )
 AXES = "zyxc"
 
@@ -789,40 +789,38 @@
     ff_down(3)
     close()
     reduce_grad(3)
-    scatter(0)
     reduce_grad(2)
     reduce_grad(1)
     reduce_grad(0)
-    scatter(2)
+    scatter(0, 2, 1)
     ff_back(3)
     ff_back(2)
     ff_back(1)
     ff_back(0)
-    scatter(3, 0, 4, 2)
     cross_open()
-    scatter(1)
+    scatter(5, 1, 2, 0)
     cross_back(0)
     scatter(3)
     memory_grad(0)
     send_memory_grad(0)
-    scatter(4)
+    scatter(4, 5, 3)
     cross_back(1)
+    scatter(4, 2)
     memory_grad(1)
     send_memory_grad(1)
-    scatter(5, 1)
     cross_query_grad()
-    scatter(2, 6)
+    scatter(6)
     memory_weight_grad()
-    scatter(5, 7)
+    scatter(0, 6, 7, 1)
     self_open()
-    scatter(3, 4, 6, 8, 7)
+    scatter(3, 4, 7)
     self_back()
-    scatter(8, 0, 1)
     self_grads()
+    scatter(10, 9, 8, 6)
     pack_small()
-    scatter(11, 9, 6, 5, 10, 11, 10, 4, 9, 0, 2, 8, 7, 1, 11, 5, 10, 3, 6, 9, 7, 0, 8, 11, 2, 1, 4)
+    scatter(11, 2)
     input_grad()
-    scatter(9, 5, 10, 7, 8, 3, 6, 11, 9, 10, 0, 5, 2, 6, 4, 7, 8, 3, 11, 1, 10, 9)
+    scatter(9, 11, 4, 5, 8, 10, 3, 7, 0, 9, 1, 11, 10, 8, 5, 6, 0, 7, 4, 9, 2, 1, 10, 11, 8, 3, 7, 6, 5, 9, 11, 8, 10, 4, 1, 6, 2, 0, 3, 7, 9, 11, 5, 10, 8)
     for work in scatters:
         while not work.over:
             work.step()

time: 104 us -> 104 us (level)
  no operation moved by 1% of the time
where the time goes in v7:
time: 104 us; the launch traced here: 103 us
  Pallas kernels  103 us (99%)
    pallas_call x1, Pallas kernels, run_layer(): pl.pallas_call(kernel, out_shape=tuple((pltpu.VMEM(shape, dtype) for shap...  101 us

profile of v7, /device:TPU:0, one launch (start us, length us, event | category | flops | bytes accessed | tf_op | source)
XLA Modules:
  0.0 103.4 jit_solution(10874066126977413752)
XLA Ops:
  0.7 100.8 %shard_map.238 = (f32[6,16]{1,0:T(8,128)S(1)}, f32[3,16]{1,0:T(4,128)S(1)}, f32[3,16]{1,0:T(4,128)S(1)}, f32[1,16]{1,0:T(1,128)S(1)}, f32[1,64]{1,0:T(1,128)S(1)...) custom-call(s32[2]{0:T(128)} %refs_3_.1, ...), custom_call_target="tpu_custom_call" | custom-call | tf_op jit(solution)/shard_map/pallas_call | solution.py:909
  101.5 1.8 %shard_map.239 = (f32[6,16]{1,0:T(8,128)}, f32[3,16]{1,0:T(4,128)}, f32[3,16]{1,0:T(4,128)}, f32[1,16]{1,0:T(1,128)}, f32[1,64]{1,0:T(1,128)}, /*index=5*/bf16[2...) custom-call(f32[6,16]{1,0:T(8,128)S(1)} %get-tuple-element.36.refs_0, ...), custom_call_target="tpu_custom_call" | custom-call | tf_op jit(solution)/shard_map/pallas_call | solution.py:932
